TPU v7x, 32 devices: a whole 2x2x4 slice. The times are simulated.
32 devices in a mesh: pipe: 16 (over z, x, core), dp: 2 (over y).
Axes of the slice: x: 2, y: 2, z: 4, core: 2. Of those that a mesh axis runs over, the one named last changes fastest.
Arguments:
- down_weight: bfloat16 [16, 1600, 1600], P('pipe', 'dp'), may hold values from -0.15625 to 0.15625
- up_weight: bfloat16 [16, 1600, 1600], P('pipe', 'dp'), may hold values from -0.15625 to 0.15625
- down_gain: bfloat16 [16, 1600], P('pipe'), may hold values from 0.5 to 1.5
- up_gain: bfloat16 [16, 1600], P('pipe'), may hold values from 0.5 to 1.5
- down_inputs: bfloat16 [16, 2, 480, 1600], P('pipe', None, 'dp'), may hold values from -6 to 6
- up_inputs: bfloat16 [16, 2, 480, 1600], P('pipe', None, 'dp'), may hold values from -6 to 6
- down_cot: bfloat16 [16, 480, 1600], P('pipe', 'dp'), may hold values from -1.5 to 1.5
- up_cot: bfloat16 [16, 480, 1600], P('pipe', 'dp'), may hold values from -1.5 to 1.5
- target_ids: int32 [2, 480], P(None, 'dp'), may hold values from 0 to 50256, as said below
Outputs:
- weight_grad: float32 [16, 1600, 1600], P('pipe', 'dp')
- gain_grad: float32 [16, 1600], P('pipe', 'dp')
- down_input_grad: bfloat16 [16, 480, 1600], P('pipe', 'dp')
- up_input_grad: bfloat16 [16, 480, 1600], P('pipe', 'dp')
Inputs may be any that keep to these rules, and one draw needn't show every extreme that they name: `target_ids`: in each block of 240 ids of a row (the ids of one device), ids below 50256 come first and the rest equal 50256, the ignored padding id; every block holds at least 120 ids below 50256 and at least one padding id.
All inputs are finite; a program needn't handle non-finite values.
Results may differ from a plain program's by a relative error of at most 0.014.
Values may be sent and summed in bfloat16 or wider, within the bound.
No kernel may reach another device: no remote copies, remote signals or barrier semaphores. Data moves between devices by JAX's collectives and lax.ppermute only.
A program may use at most 128 MiB of HBM per device.

v0:
```python
import functools

import jax
import jax.numpy as jnp
from jax import lax
from jax.experimental import pallas as pl
from jax.experimental.pallas import tpu as pltpu
from jax.sharding import PartitionSpec as P

pad_token = 50256
gelu_coef = 0.7978845608028654
cubic_coef = 0.044715
vmem_bytes = 24 * 1024 * 1024
free = pl.CostEstimate(flops=0, bytes_accessed=0, transcendentals=0)


def shifted(shard, by):
    size = lax.axis_size("pipe")
    pairs = [(i, i + by) for i in range(size) if 0 <= i + by < size]
    return lax.ppermute(shard, "pipe", pairs)


def mirrored(shard):
    size = lax.axis_size("pipe")
    return lax.ppermute(shard, "pipe", [(i, size - 1 - i) for i in range(size)])


def swapped(shard):
    return lax.ppermute(shard, "dp", [(0, 1), (1, 0)])


def after(value, *earlier):
    return lax.optimization_barrier((value, *earlier))[0]


def gelu_slope(preact):
    tangent = jnp.tanh(gelu_coef * (preact + cubic_coef * preact * preact * preact))
    return 0.5 * (1.0 + tangent) + 0.5 * preact * (1.0 - tangent * tangent) * gelu_coef * (
        1.0 + 3.0 * cubic_coef * preact * preact
    )


def whiten(rows):
    wide = rows.astype(jnp.float32)
    centered = wide - jnp.mean(wide, axis=-1, keepdims=True)
    inv_std = lax.rsqrt(jnp.mean(centered * centered, axis=-1, keepdims=True) + 1e-05)
    return centered * inv_std, inv_std


def normalize(rows, gain):
    whitened, _ = whiten(rows)
    return (whitened * gain.astype(jnp.float32)).astype(jnp.bfloat16)


def column_pieces(width):
    step = 512
    starts = list(range(0, max(width - step // 2, 1), step))
    return [(lo, hi) for lo, hi in zip(starts, starts[1:] + [width])]


def fetch(rank_ref, own_ref, far_ref, weight, sems):
    half = own_ref.shape[0]
    rank = rank_ref[0]
    pairs = []
    for i, (lo, hi) in enumerate(column_pieces(weight.shape[1])):
        pairs.append([])
        for k, (ref, side) in enumerate(((own_ref, rank), (far_ref, 1 - rank))):
            rows = pl.ds(pl.multiple_of(side * half, half), half)
            pairs[i].append(
                pltpu.make_async_copy(ref.at[:, lo:hi], weight.at[rows, lo:hi], sems.at[i, k])
            )
    for pair in pairs:
        for copy in pair:
            copy.start()
    return pairs


def wait_for(pair):
    for copy in pair:
        copy.wait()


def slope_piece(normed_ref, weight, lo, hi):
    return gelu_slope(
        jnp.dot(normed_ref[...], weight[:, lo:hi], preferred_element_type=jnp.float32)
    )


def slope_kernel(rank_ref, normed_ref, own_ref, far_ref, slope_ref, weight, sems):
    pairs = fetch(rank_ref, own_ref, far_ref, weight, sems)
    for pair, (lo, hi) in zip(pairs, column_pieces(slope_ref.shape[1])):
        wait_for(pair)
        slope_ref[:, lo:hi] = slope_piece(normed_ref, weight, lo, hi)


def fill_back(gated_ref, weight, back):
    gated = gated_ref[...]
    for lo, hi in column_pieces(weight.shape[0]):
        back[:, lo:hi] = lax.dot_general(
            gated, weight[lo:hi, :], (((1,), (1,)), ((), ())), preferred_element_type=jnp.float32
        )


def settle_back(rows_ref, cot_ref, gain_ref, back, passed_ref, term_ref):
    whitened, inv_std = whiten(rows_ref[...])
    term_ref[...] = jnp.sum(back[...] * whitened, axis=0, keepdims=True)
    scaled = back[...] * gain_ref[...].astype(jnp.float32)
    mean_back = jnp.mean(scaled, axis=-1, keepdims=True)
    mean_cross = jnp.mean(scaled * whitened, axis=-1, keepdims=True)
    passed_ref[...] = (
        cot_ref[...].astype(jnp.float32) + inv_std * (scaled - mean_back - whitened * mean_cross)
    ).astype(jnp.bfloat16)


def back_kernel(
    rank_ref, rows_ref, cot_ref, gain_ref, gated_ref, own_ref, far_ref,
    passed_ref, term_ref, weight, sems, back,
):
    for pair in fetch(rank_ref, own_ref, far_ref, weight, sems):
        wait_for(pair)
    fill_back(gated_ref, weight, back)
    settle_back(rows_ref, cot_ref, gain_ref, back, passed_ref, term_ref)


def step_kernel(
    rank_ref, rows_ref, normed_ref, cot_ref, gain_ref, own_ref, far_ref,
    gated_ref, passed_ref, term_ref, weight, sems, back,
):
    pairs = fetch(rank_ref, own_ref, far_ref, weight, sems)
    for pair, (lo, hi) in zip(pairs, column_pieces(gated_ref.shape[1])):
        wait_for(pair)
        slope = slope_piece(normed_ref, weight, lo, hi)
        gated_ref[:, lo:hi] = (cot_ref[:, lo:hi].astype(jnp.float32) * slope).astype(jnp.bfloat16)
    fill_back(gated_ref, weight, back)
    settle_back(rows_ref, cot_ref, gain_ref, back, passed_ref, term_ref)


def section_call(kernel, rank, operands, halves, outs, cost):
    tokens, width = operands[0].shape
    in_vmem = pl.BlockSpec(memory_space=pltpu.VMEM)
    shapes = {
        "rows": jax.ShapeDtypeStruct((tokens, width), jnp.bfloat16),
        "slope": jax.ShapeDtypeStruct((tokens, width), jnp.float32),
        "term": jax.ShapeDtypeStruct((1, width), jnp.float32),
    }
    scratch = [
        pltpu.VMEM((width, width), jnp.bfloat16),
        pltpu.SemaphoreType.DMA((len(column_pieces(width)), 2)),
    ]
    if "term" in outs:
        scratch.append(pltpu.VMEM((tokens, width), jnp.float32))
    return pl.pallas_call(
        kernel,
        out_shape=[shapes[out] for out in outs],
        in_specs=[pl.BlockSpec(memory_space=pltpu.SMEM)]
        + [in_vmem] * len(operands)
        + [pl.BlockSpec(memory_space=pl.ANY)] * 2,
        out_specs=[in_vmem] * len(outs),
        scratch_shapes=scratch,
        compiler_params=pltpu.CompilerParams(vmem_limit_bytes=vmem_bytes),
        cost_estimate=cost,
    )(rank, *operands, *halves)


def slope_of(rank, normed, halves, cost=free):
    return section_call(slope_kernel, rank, (normed,), halves, ["slope"], cost)[0]


def back(rank, rows, cot, gain, gated, halves, cost=free):
    return section_call(
        back_kernel, rank, (rows, cot, gain, gated), halves, ["rows", "term"], cost
    )


def whole_step(rank, rows, normed, cot, gain, halves, cost=free):
    return section_call(
        step_kernel, rank, (rows, normed, cot, gain), halves, ["rows", "rows", "term"], cost
    )


def gated_by(cot, slope):
    return (cot.astype(jnp.float32) * slope).astype(jnp.bfloat16)


def product(normed, gated):
    return lax.dot_general(
        normed, gated, (((0,), (0,)), ((), ())), preferred_element_type=jnp.float32
    )


def first_cots(down_cot, up_cot, target_ids):
    pipe_count = lax.axis_size("pipe")
    position = lax.axis_index("pipe")
    keep_down = jnp.logical_or(position != pipe_count - 1, target_ids[0] != pad_token)
    keep_up = jnp.logical_or(position != 0, target_ids[1] != pad_token)
    return (
        jnp.where(keep_down[:, None], down_cot[0], jnp.zeros_like(down_cot[0])),
        jnp.where(keep_up[:, None], up_cot[0], jnp.zeros_like(up_cot[0])),
    )


def gate_many(normed, cot, halves):
    rows = halves[0].shape[0]
    pre = sum(
        jnp.dot(normed[:, i * rows : (i + 1) * rows], half, preferred_element_type=jnp.float32)
        for i, half in enumerate(halves)
    )
    return (cot.astype(jnp.float32) * gelu_slope(pre)).astype(jnp.bfloat16)


def back_many(rows, cot, gated, halves, gain):
    whitened, inv_std = whiten(rows)
    back = jnp.concatenate(
        [
            lax.dot_general(gated, half, (((1,), (1,)), ((), ())), preferred_element_type=jnp.float32)
            for half in halves
        ],
        axis=1,
    )
    scaled = back * gain.astype(jnp.float32)
    mean_back = jnp.mean(scaled, axis=-1, keepdims=True)
    mean_cross = jnp.mean(scaled * whitened, axis=-1, keepdims=True)
    passed = (
        cot.astype(jnp.float32) + inv_std * (scaled - mean_back - whitened * mean_cross)
    ).astype(jnp.bfloat16)
    return passed, jnp.sum(back * whitened, axis=0)


def chain(inputs, cot, halves, gain, normed, by, send_gated):
    gain_term = 0.0
    gates = []
    steps = inputs.shape[0]
    for step in range(steps):
        gated = gate_many(normed[step], cot, halves)
        gates.append(send_gated(gated))
        passed, term = back_many(inputs[step], cot, gated, halves, gain)
        gain_term = gain_term + term
        cot = shifted(passed, by) if step + 1 < steps else passed
    return cot, gates, gain_term


def lanes(span):
    return -(-span // 128) * 128


def column_chunks(width):
    lane = 128
    tiles = -(-width // lane)
    first = -(-tiles // 2)
    second = first + (tiles - first) // 2
    edges = [0, first * lane, second * lane, width]
    return list(zip(edges, edges[1:]))


def gather_gates(gate_refs, lo, span, stack, sems):
    copies = []
    row = 0
    for k, ref in enumerate(gate_refs):
        rows, width = ref.shape
        source = ref if width == span else ref.at[:, lo : lo + span]
        copies.append(
            pltpu.make_async_copy(source, stack.at[row : row + rows, :], sems.at[k])
        )
        row += rows
    for copy in copies:
        copy.start()
    for copy in copies:
        copy.wait()


def send_kernel(lo, span, rank_ref, turned_ref, *refs):
    *gate_refs, part_ref, stack, sems = refs

    @pl.when(pl.program_id(0) == 0)
    def _():
        gather_gates(gate_refs, lo, span, stack, sems)

    part_ref[:, :span] = jnp.dot(
        turned_ref[...], stack[...], preferred_element_type=jnp.float32
    ).astype(jnp.bfloat16)
    if span < part_ref.shape[1]:
        spare = (part_ref.shape[0], part_ref.shape[1] - span)
        part_ref[:, span:] = jnp.zeros(spare, jnp.bfloat16)


def keep_kernel(lo, span, count, grown, rank_ref, turned_ref, arrived_ref, *refs):
    gate_refs = refs[:count]
    out_ref, stack, total, sems, out_sems = refs[count + (1 if grown else 0) :]
    step = pl.program_id(0)
    rows = total.shape[1]

    @pl.when(step == 0)
    def _():
        gather_gates(gate_refs, lo, span, stack, sems)

    total[step] = jnp.dot(
        turned_ref[...], stack[...], preferred_element_type=jnp.float32
    ) + arrived_ref[:, :span].astype(jnp.float32)

    def put(i):
        return pltpu.make_async_copy(
            total.at[i], out_ref.at[pl.ds(i * rows, rows), lo : lo + span], out_sems.at[i]
        )

    put(step).start()

    @pl.when(step == pl.num_programs(0) - 1)
    def _():
        for i in range(total.shape[0]):
            put(i).wait()


def product_call(rank, turned, gates, lo, hi, arrived=None, grown=None):
    width, depth = turned.shape
    half, span = width // 2, hi - lo
    padded = lanes(span)
    blocks = 2 if half % 32 == 0 else 1
    rows = half // blocks
    sending = arrived is None
    any_space = pl.BlockSpec(memory_space=pl.ANY)

    def turned_at(i, rank_ref):
        side = 1 - rank_ref[0] if sending else rank_ref[0]
        return side * blocks + i, 0

    in_specs = [pl.BlockSpec((rows, depth), turned_at)]
    operands = [turned]
    if not sending:
        in_specs.append(pl.BlockSpec((rows, padded), lambda i, rank_ref: (i, 0)))
        operands.append(arrived)
    in_specs += [any_space] * len(gates)
    operands += gates
    scratch = [pltpu.VMEM((depth, span), jnp.bfloat16)]
    aliases = {}
    if sending:
        kernel = functools.partial(send_kernel, lo, span)
        out_shape = jax.ShapeDtypeStruct((half, padded), jnp.bfloat16)
        out_spec = pl.BlockSpec((rows, padded), lambda i, rank_ref: (i, 0))
        scratch += [pltpu.SemaphoreType.DMA((len(gates),))]
    else:
        kernel = functools.partial(keep_kernel, lo, span, len(gates), grown is not None)
        out_shape = jax.ShapeDtypeStruct((half, width), jnp.float32)
        out_spec = any_space
        scratch += [
            pltpu.VMEM((blocks, rows, span), jnp.float32),
            pltpu.SemaphoreType.DMA((len(gates),)),
            pltpu.SemaphoreType.DMA((blocks,)),
        ]
        if grown is not None:
            aliases = {1 + len(operands): 0}
            in_specs.append(any_space)
            operands.append(grown)
    return pl.pallas_call(
        kernel,
        out_shape=out_shape,
        grid_spec=pltpu.PrefetchScalarGridSpec(
            num_scalar_prefetch=1,
            grid=(blocks,),
            in_specs=in_specs,
            out_specs=out_spec,
            scratch_shapes=scratch,
        ),
        input_output_aliases=aliases,
        compiler_params=pltpu.CompilerParams(vmem_limit_bytes=vmem_bytes),
        cost_estimate=pl.CostEstimate(
            flops=2 * half * depth * span,
            bytes_accessed=4 * half * depth + 8 * half * span,
            transcendentals=0,
        ),
    )(rank, *operands)


def local_pair(
    down_weight, up_weight, down_gain, up_gain, down_inputs, up_inputs, down_cot, up_cot, target_ids
):
    rank_index = lax.axis_index("dp")
    first = rank_index == 0
    rank = rank_index.astype(jnp.int32)[None]
    half, width = down_weight.shape[1:]
    steps = down_inputs.shape[1]

    up_far = swapped(up_weight[0])
    normed_up = normalize(up_inputs[0], up_gain[0])
    normed_moved = mirrored(normed_up)
    cot_down, cot_up = first_cots(down_cot, up_cot, target_ids)
    down_far = swapped(after(down_weight[0], normed_up, cot_up))

    halves_up = (up_weight[0], up_far)
    gated_up = []
    up_term = 0.0
    down_rows = down_inputs[0]
    for step in range(steps - 1):
        gated, passed, term = whole_step(
            rank, up_inputs[0, step], normed_up[step], cot_up, up_gain, halves_up
        )
        gated_up.append(gated)
        up_term = up_term + term
        cot_up = shifted(passed, 1)
        down_rows, cot_down = lax.optimization_barrier((down_rows, cot_down, passed))[:2]
        normed_down = [normalize(rows, down_gain[0]) for rows in down_rows]
    slope_up = slope_of(rank, after(normed_up[-1], passed), halves_up)
    gated_up.append(gated_by(after(cot_up, slope_up), slope_up))
    chunks = column_chunks(width)

    def columns(gates, lo, hi):
        return jnp.concatenate([gated[:, lo:hi] for gated in gates], axis=0)

    moved = [mirrored(columns(gated_up, *chunks[0]))]
    up_last, term = back(
        rank, up_inputs[0, -1], cot_up, up_gain, gated_up[-1], halves_up
    )
    mirror_term = mirrored((up_term + term).astype(jnp.bfloat16))
    turned = jnp.concatenate([*normed_down, *after(normed_moved, slope_up)], axis=0).T

    down_far, turned = lax.optimization_barrier((down_far, turned, up_last))[:2]
    halves_down = (down_weight[0], down_far)
    gated_down = []
    down_term = 0.0
    for step in range(steps - 1):
        gated, passed, term = whole_step(
            rank, down_inputs[0, step], normed_down[step], cot_down, down_gain, halves_down
        )
        gated_down.append(gated)
        down_term = down_term + term
        cot_down = shifted(passed, -1)
    slope_down = slope_of(rank, after(normed_down[-1], passed, moved), halves_down)
    gated_down.append(gated_by(after(cot_down, slope_down), slope_down))

    arrived = []
    gates = []
    part = gated_down[-1]
    for i, (lo, hi) in enumerate(chunks):
        if i > 0:
            source = after(gated_up, cot_down if i == 1 else part)
            moved.append(mirrored(columns(source, lo, hi)))
        ready = [part] + arrived[max(i - 2, 0) : max(i - 1, 0)]
        gates.append(gated_down + [after(moved[i], *ready)])
        part = product_call(rank, turned, gates[i], lo, hi)
        arrived.append(swapped(part))
        if i == 0:
            down_last, term = back(
                rank, down_inputs[0, -1], cot_down, down_gain, after(gated_down[-1], part),
                halves_down,
            )
            gain_sum = (down_term + term + mirror_term.astype(jnp.float32))[0]
            gain_keep = jnp.where(first, gain_sum[:half], gain_sum[half:])
            gain_send = jnp.where(first, gain_sum[half:], gain_sum[:half])
            gain_got = swapped(gain_send.astype(jnp.bfloat16))
    weight_out = None
    for i, (lo, hi) in enumerate(chunks):
        if i == len(chunks) - 1:
            gain_got = after(gain_got, weight_out)
        weight_out = product_call(rank, turned, gates[i], lo, hi, arrived[i], weight_out)
    gain_out = gain_keep + gain_got.astype(jnp.float32)
    return (weight_out[None], gain_out[None], down_last[None], up_last[None])


def local_many(
    down_weight, up_weight, down_gain, up_gain, down_inputs, up_inputs, down_cot, up_cot, target_ids
):
    halves_up = (lax.all_gather(up_weight[0], "dp", axis=0, tiled=True),)
    halves_down = (lax.all_gather(down_weight[0], "dp", axis=0, tiled=True),)
    normed_up = [normalize(rows, up_gain[0]) for rows in up_inputs[0]]
    normed_down = [normalize(rows, down_gain[0]) for rows in down_inputs[0]]
    moved_normed = [mirrored(normed) for normed in normed_up]
    start_down, start_up = first_cots(down_cot, up_cot, target_ids)
    up_last, moved_gated, up_gain_term = chain(
        up_inputs[0], start_up, halves_up, up_gain[0], normed_up, 1, mirrored
    )
    up_gain_moved = mirrored(up_gain_term.astype(jnp.bfloat16))
    down_last, gated_down, down_gain_term = chain(
        down_inputs[0], start_down, halves_down, down_gain[0], normed_down, -1, lambda gated: gated
    )
    normed = jnp.concatenate(normed_down + moved_normed, axis=0)
    gated = jnp.concatenate(gated_down + moved_gated, axis=0)
    gain_sum = down_gain_term + up_gain_moved.astype(jnp.float32)

    def settle(values):
        return lax.psum_scatter(
            values.astype(jnp.bfloat16), "dp", scatter_dimension=0, tiled=True
        ).astype(jnp.float32)

    return (
        settle(product(normed, gated))[None],
        settle(gain_sum)[None],
        down_last[None],
        up_last[None],
    )


def solution(mesh):
    placed = (
        P("pipe", "dp", None),
        P("pipe", "dp", None),
        P("pipe", None),
        P("pipe", None),
        P("pipe", None, "dp", None),
        P("pipe", None, "dp", None),
        P("pipe", "dp", None),
        P("pipe", "dp", None),
        P(None, "dp"),
    )
    return jax.shard_map(
        local_pair if mesh.shape["dp"] == 2 else local_many,
        mesh=mesh,
        in_specs=placed,
        out_specs=(
            P("pipe", "dp", None),
            P("pipe", "dp"),
            P("pipe", "dp", None),
            P("pipe", "dp", None),
        ),
        check_vma=False,
    )
```

profile of v0, /device:TPU:15, one launch (start us, length us, event | category | flops | bytes accessed | tf_op | source)
XLA Modules:
  0.0 207.7 jit_solution(13567702855330181358)
XLA Ops:
  0.9 1.9 convert_reduce_fusion
  2.8 0.6 fusion.3
  3.5 1.7 fusion.5
  5.2 2.0 collective-permute-start.2
  7.2 2.5 %bitcast_select_fusion = (bf16[240,1600]{1,0:T(8,128)(2,1)}, bf16[240,1600]{1,0:T(8,128)(2,1)S(1)}) fusion(bf16[1,240,1600]{2,1,0:T(8,128)(2,1)} %param.15, pred[240]{0:T(512)(128)(4,1)S(1)} %get-tuple-element.66, bf16[1,240,1600]{2,1,0:T(8,128)(2,1)} %param.16, pred[240]{0:T(512)(128)(4,1)S(1)} %get-tuple-element.67), kind=kLoop, calls=%fused_computation.32 | loop fusion | flops 768000 | bytes 3072480 | tf_op jit(solution)/shard_map/jit(_where)/select_n | solution.py:197
  9.6 1.2 collective-permute-start
  10.9 3.6 %copy.21 = bf16[1,2,240,1600]{2,3,1,0:T(8,128)(2,1)} copy(bf16[1,2,240,1600]{3,2,1,0:T(8,128)(2,1)} %param.13) | data formatting | bytes 3072000 | tf_op args[4]
  14.5 1.6 slice_bitcast_fusion.3
  16.3 1.3 slice_bitcast_fusion.4
  17.6 0.7 copy-done.28
  18.3 1.0 slice_bitcast_fusion.6
  19.3 40.3 %collective-permute-done.1.far_ref = bf16[800,1600]{1,0:T(8,128)(2,1)S(1)} collective-permute-done((bf16[800,1600]{1,0:T(8,128)(2,1)}, bf16[800,1600]{1,0:T(8,128)(2,1)S(1)}, u32[]{:S(2)}, u32[]{:S(2)}) %collective-permute-start.1) | collective-permute-done | bytes 2560032 | tf_op jit(solution)/shard_map/ppermute | solution.py:29
  59.6 6.7 %shard_map.120 = (bf16[240,1600]{1,0:T(8,128)(2,1)S(1)}, bf16[240,1600]{1,0:T(8,128)(2,1)}, f32[1,1600]{1,0:T(1,128)S(1)}) custom-call(s32[1]{0:T(128)} %bitcast.rank_ref, bf16[240,1600]{1,0:T(8,128)(2,1)S(1)} %get-tuple-element.75.rows_ref, bf16[240,1600]{1,0:T(8,128)(2,1)S(1)} %get-tuple-element.76.normed_ref, ...), custom_call_target="tpu_custom_call" | custom-call | tf_op jit(solution)/shard_map/pallas_call | solution.py:152
  66.3 5.8 %collective-permute-start.3 = (bf16[240,1600]{1,0:T(8,128)(2,1)}, bf16[240,1600]{1,0:T(8,128)(2,1)S(1)}, u32[]{:S(2)}, u32[]{:S(2)}) collective-permute-start(bf16[240,1600]{1,0:T(8,128)(2,1)} %get-tuple-element.34), channel_id=1, source_target_pairs={{0,2},{2,4},{4,6},{6,8},{8,10},{10,12},{12,14},{14,16},{16,18},{18... | collective-permute-start | bytes 2304008 | tf_op jit(solution)/shard_map/ppermute | solution.py:20
  72.2 3.3 %shard_map.121 = f32[240,1600]{1,0:T(8,128)S(1)} custom-call(s32[1]{0:T(128)} %bitcast.rank_ref, bf16[240,1600]{1,0:T(8,128)(2,1)S(1)} %get-tuple-element.36.normed_ref, bf16[800,1600]{1,0:T(8,128)(2,1)S(1)} %bitcast.73, bf16[800,1600]{1,0:T(8,128)(2,1)S(1)} %collective-permute-done.1.far_ref), custom_call_target="tpu_custom_call" | custom-call | tf_op jit(solution)/shard_map/pallas_call | solution.py:152
  75.5 1.2 copy-done.11
  76.7 0.3 convert_reduce_fusion.2
  77.0 1.0 collective-permute-done.2
  78.1 3.6 %copy.22 = bf16[2,240,1600]{1,2,0:T(8,128)(2,1)} copy(bf16[2,240,1600]{2,1,0:T(8,128)(2,1)} %collective-permute-done.2) | data formatting | bytes 3072000 | tf_op jit(solution)/shard_map/optimization_barrier | solution.py:33
  81.6 0.5 fusion.9
  82.1 0.9 copy-done.31
  83.2 1.0 copy-done.22
  84.3 0.5 fusion.11
  84.9 0.8 copy-done.12
  85.9 0.8 copy-done.18
  86.6 1.0 pad_maximum_fusion
  87.6 2.5 %collective-permute-start.5 = (bf16[480,896]{1,0:T(8,128)(2,1)}, bf16[480,896]{1,0:T(8,128)(2,1)}, u32[]{:S(2)}, u32[]{:S(2)}) collective-permute-start(bf16[480,896]{1,0:T(8,128)(2,1)} %pad_maximum_fusion), channel_id=1, source_target_pairs={{0,30},{2,28},{4,26},{6,24},{8,22},{10,20},{12,18},{14,16},{16,14}... | collective-permute-start | bytes 2580488 | tf_op jit(solution)/shard_map/ppermute | solution.py:25
  90.1 2.4 %maximum_bitcast_fusion.turned_ref = bf16[1600,960]{1,0:T(8,128)(2,1)S(1)} fusion(bf16[240,1600]{0,1:T(8,128)(2,1)S(1)} %get-tuple-element.71, bf16[240,1600]{0,1:T(8,128)(2,1)S(1)} %get-tuple-element.70, bf16[240,1600]{0,1:T(8,128)(2,1)S(1)} %get-tuple-element.46, bf16[240,1600]{0,1:T(8,128)(2,1)S(1)} %get-tuple-element.68), kind=kLoop, calls=%fused_computation.2 | loop fusion | flops 12288000 | bytes 6144000 | tf_op jit(solution)/shard_map/transpose | solution.py:413
  92.4 2.2 %copy.24.normed_ref = bf16[240,1600]{1,0:T(8,128)(2,1)} copy(bf16[240,1600]{0,1:T(8,128)(2,1)} %copy-done.30) | data formatting | bytes 1536000 | tf_op jit(solution)/shard_map/convert_element_type | solution.py:52
  94.6 1.7 copy-done.6
  96.4 1.7 copy-done.8
  98.1 1.1 copy-done.10
  99.3 1.1 copy-done.17
  100.4 1.1 copy-done.19
  101.6 4.1 %shard_map.122 = (bf16[240,1600]{1,0:T(8,128)(2,1)}, f32[1,1600]{1,0:T(1,128)S(1)}) custom-call(s32[1]{0:T(128)} %bitcast.rank_ref, bf16[240,1600]{1,0:T(8,128)(2,1)S(1)} %copy-done.17, bf16[240,1600]{1,0:T(8,128)(2,1)S(1)} %copy-done.19, bf16[1,1600]{1,0:T(2,128)(2,1)S(1)} %copy-done.23, bf16[240,1600]{1,0:T(8,128)(2,1)S(1)} %copy-done.10, ...), custom_call_target="tpu_custom_call" | custom-call | tf_op jit(solution)/shard_map/pallas_call | solution.py:152
  105.7 11.0 %collective-permute-done.far_ref = bf16[800,1600]{1,0:T(8,128)(2,1)} collective-permute-done((bf16[800,1600]{1,0:T(8,128)(2,1)}, bf16[800,1600]{1,0:T(8,128)(2,1)}, u32[]{:S(2)}, u32[]{:S(2)}) %collective-permute-start) | collective-permute-done | bytes 2560032 | tf_op jit(solution)/shard_map/ppermute | solution.py:29
  116.7 7.6 %shard_map.123 = (bf16[240,1600]{1,0:T(8,128)(2,1)S(1)}, bf16[240,1600]{1,0:T(8,128)(2,1)}, f32[1,1600]{1,0:T(1,128)S(1)}) custom-call(s32[1]{0:T(128)} %bitcast.rank_ref, bf16[240,1600]{1,0:T(8,128)(2,1)S(1)} %copy-done.16, bf16[240,1600]{1,0:T(8,128)(2,1)S(1)} %copy-done.20, bf16[240,1600]{1,0:T(8,128)(2,1)S(1)} %copy-done.15, ...), custom_call_target="tpu_custom_call" | custom-call | tf_op jit(solution)/shard_map/pallas_call | solution.py:152
  124.3 0.9 copy-done.2
  125.2 3.4 %collective-permute-start.4 = (bf16[240,1600]{1,0:T(8,128)(2,1)}, bf16[240,1600]{1,0:T(8,128)(2,1)}, u32[]{:S(2)}, u32[]{:S(2)}) collective-permute-start(bf16[240,1600]{1,0:T(8,128)(2,1)} %get-tuple-element.44), channel_id=1, source_target_pairs={{2,0},{4,2},{6,4},{8,6},{10,8},{12,10},{14,12},{16,14},{18,16},{20... | collective-permute-start | bytes 2304008 | tf_op jit(solution)/shard_map/ppermute | solution.py:20
  128.7 2.5 %copy.25.normed_ref = bf16[240,1600]{1,0:T(8,128)(2,1)} copy(bf16[240,1600]{0,1:T(8,128)(2,1)} %copy-done.29) | data formatting | bytes 1536000 | tf_op jit(solution)/shard_map/optimization_barrier | solution.py:33
  131.1 1.1 copy-done.13
  132.3 4.2 %shard_map.124 = f32[240,1600]{1,0:T(8,128)S(1)} custom-call(s32[1]{0:T(128)} %bitcast.rank_ref, bf16[240,1600]{1,0:T(8,128)(2,1)S(1)} %copy-done.13, bf16[800,1600]{1,0:T(8,128)(2,1)} %bitcast.1.own_ref, bf16[800,1600]{1,0:T(8,128)(2,1)} %collective-permute-done.far_ref), custom_call_target="tpu_custom_call" | custom-call | tf_op jit(solution)/shard_map/pallas_call | solution.py:152
  136.5 3.4 %collective-permute-done.4.cot_ref = bf16[240,1600]{1,0:T(8,128)(2,1)} collective-permute-done((bf16[240,1600]{1,0:T(8,128)(2,1)}, bf16[240,1600]{1,0:T(8,128)(2,1)}, u32[]{:S(2)}, u32[]{:S(2)}) %collective-permute-start.4) | collective-permute-done | bytes 768032 | tf_op jit(solution)/shard_map/ppermute | solution.py:20
  139.9 1.3 multiply_convert_fusion.refs_1_.gated_ref
  141.2 4.5 %shard_map.125 = bf16[800,896]{1,0:T(8,128)(2,1)} custom-call(s32[1]{0:T(128)} %bitcast.rank_ref, bf16[1600,960]{1,0:T(8,128)(2,1)S(1)} %maximum_bitcast_fusion.turned_ref, bf16[240,1600]{1,0:T(8,128)(2,1)S(1)} %copy-done.3, bf16[240,1600]{1,0:T(8,128)(2,1)S(1)} %multiply_convert_fusion.refs_1_.gated_ref, bf16[480,896]{1,0:T(8,128)(2,1)} %collective-permute-done.5.refs_2_), custom_call_target="tpu_custom_call" | custom-call | flops 1376256000 | bytes 8806400 | tf_op jit(solution)/shard_map/pallas_call | solution.py:353
  146.0 1.0 slice.61
  147.3 2.6 %collective-permute-start.11 = (bf16[1,1600]{1,0:T(2,128)(2,1)S(1)}, bf16[1,1600]{1,0:T(2,128)(2,1)S(1)}, u32[]{:S(2)}, u32[]{:S(2)}) collective-permute-start(bf16[1,1600]{1,0:T(2,128)(2,1)S(1)} %add_convert_fusion), channel_id=1, source_target_pairs={{0,30},{2,28},{4,26},{6,24},{8,22},{10,20},{12,18},{14,16},{16,14}... | collective-permute-start | bytes 9608 | tf_op jit(solution)/shard_map/ppermute | solution.py:25
  149.9 1.1 copy-done.14
  151.0 7.2 %shard_map.131 = (bf16[240,1600]{1,0:T(8,128)(2,1)}, f32[1,1600]{1,0:T(1,128)S(1)}) custom-call(s32[1]{0:T(128)} %bitcast.rank_ref, bf16[240,1600]{1,0:T(8,128)(2,1)S(1)} %copy-done.14, bf16[240,1600]{1,0:T(8,128)(2,1)} %collective-permute-done.4.cot_ref, bf16[1,1600]{1,0:T(2,128)(2,1)S(1)} %copy-done.24, bf16[240,1600]{1,0:T(8,128)(2,1)S(1)} %copy-done.1, ...), custom_call_target="tpu_custom_call" | custom-call | tf_op jit(solution)/shard_map/pallas_call | solution.py:152
  158.2 7.1 %collective-permute-done.6.refs_2_ = bf16[480,384]{1,0:T(8,128)(2,1)S(1)} collective-permute-done((bf16[480,384]{1,0:T(8,128)(2,1)S(1)}, bf16[480,384]{1,0:T(8,128)(2,1)S(1)}, u32[]{:S(2)}, u32[]{:S(2)}) %collective-permute-start.6) | collective-permute-done | bytes 368672 | tf_op jit(solution)/shard_map/ppermute | solution.py:25
  165.3 1.4 shard_map.126
  166.8 1.3 collective-permute-start.10
  168.1 0.9 slice.63
  169.1 0.4 collective-permute-start.7
  169.5 13.8 %collective-permute-done.7.refs_2_ = bf16[480,320]{1,0:T(8,128)(2,1)S(1)} collective-permute-done((bf16[480,320]{1,0:T(8,128)(2,1)S(1)}, bf16[480,320]{1,0:T(8,128)(2,1)S(1)}, u32[]{:S(2)}, u32[]{:S(2)}) %collective-permute-start.7) | collective-permute-done | bytes 307232 | tf_op jit(solution)/shard_map/ppermute | solution.py:25
  183.3 1.4 shard_map.127
  184.7 0.3 collective-permute-start.9
  185.1 1.3 collective-permute-start.12
  186.5 5.6 %shard_map.128.refs_3_ = f32[800,1600]{1,0:T(8,128)} custom-call(s32[1]{0:T(128)} %bitcast.rank_ref, bf16[1600,960]{1,0:T(8,128)(2,1)S(1)} %maximum_bitcast_fusion.turned_ref, bf16[800,896]{1,0:T(8,128)(2,1)} %collective-permute-done.8.arrived_ref, bf16[240,1600]{1,0:T(8,128)(2,1)S(1)} %copy-done.4, bf16[240,1600]{1,0:T(8,128)(2,1)S(1)} %copy-done.1, ...), custom_call_target="tpu_custom_call" | custom-call | flops 1376256000 | bytes 8806400 | tf_op jit(solution)/shard_map/pallas_call | solution.py:353
  192.1 0.5 collective-permute-done.10.arrived_ref
  192.6 2.3 %shard_map.129.refs_3_ = f32[800,1600]{1,0:T(8,128)} custom-call(s32[1]{0:T(128)} %bitcast.rank_ref, bf16[1600,960]{1,0:T(8,128)(2,1)S(1)} %maximum_bitcast_fusion.turned_ref, bf16[800,384]{1,0:T(8,128)(2,1)S(1)} %collective-permute-done.10.arrived_ref, bf16[240,1600]{1,0:T(8,128)(2,1)S(1)} %copy-done.4, ...), custom_call_target="tpu_custom_call", output_to_operand_aliasing={{}: (6, {})} | custom-call | flops 589824000 | bytes 5529600 | tf_op jit(solution)/shard_map/pallas_call | solution.py:353
  194.8 9.8 %collective-permute-done.12 = bf16[800]{0:T(1024)(128)(2,1)S(1)} collective-permute-done((bf16[800]{0:T(1024)(128)(2,1)S(1)}, bf16[800]{0:T(1024)(128)(2,1)S(1)}, u32[]{:S(2)}, u32[]{:S(2)}) %collective-permute-start.12) | collective-permute-done | bytes 1632 | tf_op jit(solution)/shard_map/ppermute | solution.py:29
  204.6 0.6 broadcast_in_dim.43
  205.2 2.3 %shard_map.130 = f32[800,1600]{1,0:T(8,128)} custom-call(s32[1]{0:T(128)} %bitcast.rank_ref, bf16[1600,960]{1,0:T(8,128)(2,1)S(1)} %maximum_bitcast_fusion.turned_ref, bf16[800,384]{1,0:T(8,128)(2,1)S(1)} %collective-permute-done.9.arrived_ref, bf16[240,1600]{1,0:T(8,128)(2,1)S(1)} %copy-done.4, ...), custom_call_target="tpu_custom_call", output_to_operand_aliasing={{}: (6, {})} | custom-call | flops 491520000 | bytes 5120000 | tf_op jit(solution)/shard_map/pallas_call | solution.py:353
  (86 shorter events, 1.9 us)
Async XLA Ops:
  0.6 2.2 %copy-start.27 = (bf16[1,2,240,1600]{3,2,1,0:T(8,128)(2,1)S(1)}, bf16[1,2,240,1600]{3,2,1,0:T(8,128)(2,1)}, u32[]{:S(2)}) copy-start(bf16[1,2,240,1600]{3,2,1,0:T(8,128)(2,1)} %param.14) | copy-start | bytes 4608004
  0.6 2.8 %copy-start.23 = (bf16[1,1600]{1,0:T(2,128)(2,1)S(1)}, bf16[1,1600]{1,0:T(2,128)(2,1)}, u32[]{:S(2)}) copy-start(bf16[1,1600]{1,0:T(2,128)(2,1)} %gain_ref.5) | copy-start | bytes 9604
  0.7 59.0 %collective-permute-start.1 = (bf16[800,1600]{1,0:T(8,128)(2,1)}, bf16[800,1600]{1,0:T(8,128)(2,1)S(1)}, u32[]{:S(2)}, u32[]{:S(2)}) collective-permute-start(bf16[800,1600]{1,0:T(8,128)(2,1)} %bitcast.71), channel_id=1, source_target_pairs={{0,1},{1,0},{2,3},{3,2},{4,5},{5,4},{6,7},{7,6},{8,9},{9,8},{10,11... | collective-permute-start | bytes 7680008 | tf_op jit(solution)/shard_map/ppermute | solution.py:29
  3.4 3.7 %copy-start.33 = (s32[2,240]{1,0:T(2,128)S(1)}, s32[2,240]{1,0:T(2,128)}, u32[]{:S(2)}) copy-start(s32[2,240]{1,0:T(2,128)} %param.17) | copy-start | bytes 5764
  5.2 72.9 %collective-permute-start.2 = (bf16[2,240,1600]{2,1,0:T(8,128)(2,1)}, bf16[2,240,1600]{2,1,0:T(8,128)(2,1)}, u32[]{:S(2)}, u32[]{:S(2)}) collective-permute-start(bf16[2,240,1600]{2,1,0:T(8,128)(2,1)} %fusion.5), channel_id=1, source_target_pairs={{0,30},{2,28},{4,26},{6,24},{8,22},{10,20},{12,18},{14,16},{16,14}... | collective-permute-start | bytes 4608008 | tf_op jit(solution)/shard_map/ppermute | solution.py:25
  9.6 4.8 %copy-start.24 = (bf16[1,1600]{1,0:T(2,128)(2,1)S(1)}, bf16[1,1600]{1,0:T(2,128)(2,1)}, u32[]{:S(2)}) copy-start(bf16[1,1600]{1,0:T(2,128)(2,1)} %gain_ref.7) | copy-start | bytes 9604
  9.6 107.1 %collective-permute-start = (bf16[800,1600]{1,0:T(8,128)(2,1)}, bf16[800,1600]{1,0:T(8,128)(2,1)}, u32[]{:S(2)}, u32[]{:S(2)}) collective-permute-start(bf16[800,1600]{1,0:T(8,128)(2,1)} %bitcast.1.own_ref), channel_id=1, source_target_pairs={{0,1},{1,0},{2,3},{3,2},{4,5},{5,4},{6,7},{7,6},{8,9},{9,8},{10,11... | collective-permute-start | bytes 7680008 | tf_op jit(solution)/shard_map/ppermute | solution.py:29
  14.4 1.9 copy-start.32
  16.3 2.0 copy-start.28
  18.3 41.3 %copy-start.5 = (bf16[1,800,1600]{2,1,0:T(8,128)(2,1)S(1)}, bf16[1,800,1600]{2,1,0:T(8,128)(2,1)}, u32[]{:S(2)}) copy-start(bf16[1,800,1600]{2,1,0:T(8,128)(2,1)} %param.10) | copy-start | bytes 7680004
  59.6 12.5 %copy-start.7 = (bf16[800,1600]{1,0:T(8,128)(2,1)}, bf16[800,1600]{1,0:T(8,128)(2,1)S(1)}, u32[]{:S(2)}) copy-start(bf16[800,1600]{1,0:T(8,128)(2,1)S(1)} %collective-permute-done.1.far_ref) | copy-start | bytes 7680004
  66.3 9.1 %copy-start.21 = (bf16[240,1600]{1,0:T(8,128)(2,1)}, bf16[240,1600]{1,0:T(8,128)(2,1)S(1)}, u32[]{:S(2)}) copy-start(bf16[240,1600]{1,0:T(8,128)(2,1)S(1)} %get-tuple-element.52) | copy-start | bytes 2304004
  66.3 18.5 %collective-permute-start.3 = (bf16[240,1600]{1,0:T(8,128)(2,1)}, bf16[240,1600]{1,0:T(8,128)(2,1)S(1)}, u32[]{:S(2)}, u32[]{:S(2)}) collective-permute-start(bf16[240,1600]{1,0:T(8,128)(2,1)} %get-tuple-element.34), channel_id=1, source_target_pairs={{0,2},{2,4},{4,6},{6,8},{8,10},{10,12},{12,14},{14,16},{16,18},{18... | collective-permute-start | bytes 2304008 | tf_op jit(solution)/shard_map/ppermute | solution.py:20
  72.2 4.5 %copy-start.25 = (bf16[1,2,240,1600]{2,3,1,0:T(8,128)(2,1)S(1)}, bf16[1,2,240,1600]{2,3,1,0:T(8,128)(2,1)}, u32[]{:S(2)}) copy-start(bf16[1,2,240,1600]{2,3,1,0:T(8,128)(2,1)} %copy.21) | copy-start | bytes 4608004
  75.5 1.3 copy-start.11
  77.0 4.6 %copy-start.26 = (bf16[1,2,240,1600]{2,3,1,0:T(8,128)(2,1)S(1)}, bf16[1,2,240,1600]{2,3,1,0:T(8,128)(2,1)}, u32[]{:S(2)}) copy-start(bf16[1,2,240,1600]{2,3,1,0:T(8,128)(2,1)} %copy.21) | copy-start | bytes 4608004
  81.6 1.4 copy-start.31
  83.1 1.1 copy-start.22
  84.2 1.4 copy-start.12
  84.8 5.3 %copy-start.29 = (bf16[240,1600]{0,1:T(8,128)(2,1)}, bf16[240,1600]{0,1:T(8,128)(2,1)S(1)}, u32[]{:S(2)}) copy-start(bf16[240,1600]{0,1:T(8,128)(2,1)S(1)} %get-tuple-element.46) | copy-start | bytes 2304004
  84.8 5.3 %copy-start.30 = (bf16[240,1600]{0,1:T(8,128)(2,1)}, bf16[240,1600]{0,1:T(8,128)(2,1)S(1)}, u32[]{:S(2)}) copy-start(bf16[240,1600]{0,1:T(8,128)(2,1)S(1)} %get-tuple-element.68) | copy-start | bytes 2304004
  85.7 1.0 copy-start.18
  85.8 4.3 %copy-start.9 = (bf16[240,1600]{1,0:T(8,128)(2,1)}, bf16[240,1600]{1,0:T(8,128)(2,1)S(1)}, u32[]{:S(2)}) copy-start(bf16[240,1600]{1,0:T(8,128)(2,1)S(1)} %multiply_convert_fusion.1.gated_ref) | copy-start | bytes 2304004
  87.6 41.1 %collective-permute-start.5 = (bf16[480,896]{1,0:T(8,128)(2,1)}, bf16[480,896]{1,0:T(8,128)(2,1)}, u32[]{:S(2)}, u32[]{:S(2)}) collective-permute-start(bf16[480,896]{1,0:T(8,128)(2,1)} %pad_maximum_fusion), channel_id=1, source_target_pairs={{0,30},{2,28},{4,26},{6,24},{8,22},{10,20},{12,18},{14,16},{16,14}... | collective-permute-start | bytes 2580488 | tf_op jit(solution)/shard_map/ppermute | solution.py:25
  94.6 1.8 copy-start.6
  96.4 1.8 copy-start.8
  98.1 1.1 copy-start.10
  99.3 1.1 copy-start.17
  100.4 1.1 copy-start.19
  101.6 15.2 %copy-start.15 = (bf16[240,1600]{1,0:T(8,128)(2,1)S(1)}, bf16[240,1600]{1,0:T(8,128)(2,1)}, u32[]{:S(2)}) copy-start(bf16[240,1600]{1,0:T(8,128)(2,1)} %get-tuple-element.41.cot_ref) | copy-start | bytes 2304004
  101.6 15.2 %copy-start.16 = (bf16[240,1600]{1,0:T(8,128)(2,1)S(1)}, bf16[240,1600]{1,0:T(8,128)(2,1)}, u32[]{:S(2)}) copy-start(bf16[240,1600]{1,0:T(8,128)(2,1)} %get-tuple-element.73.rows_ref) | copy-start | bytes 2304004
  101.6 15.2 %copy-start.20 = (bf16[240,1600]{1,0:T(8,128)(2,1)S(1)}, bf16[240,1600]{1,0:T(8,128)(2,1)}, u32[]{:S(2)}) copy-start(bf16[240,1600]{1,0:T(8,128)(2,1)} %copy.24.normed_ref) | copy-start | bytes 2304004
  124.3 0.9 copy-start.2
  125.2 14.7 %collective-permute-start.4 = (bf16[240,1600]{1,0:T(8,128)(2,1)}, bf16[240,1600]{1,0:T(8,128)(2,1)}, u32[]{:S(2)}, u32[]{:S(2)}) collective-permute-start(bf16[240,1600]{1,0:T(8,128)(2,1)} %get-tuple-element.44), channel_id=1, source_target_pairs={{2,0},{4,2},{6,4},{8,6},{10,8},{12,10},{14,12},{16,14},{18,16},{20... | collective-permute-start | bytes 2304008 | tf_op jit(solution)/shard_map/ppermute | solution.py:20
  131.1 1.1 copy-start.13
  136.5 4.7 %copy-start.3 = (bf16[240,1600]{1,0:T(8,128)(2,1)S(1)}, bf16[240,1600]{1,0:T(8,128)(2,1)}, u32[]{:S(2)}) copy-start(bf16[240,1600]{1,0:T(8,128)(2,1)} %copy-done.2) | copy-start | bytes 2304004
  141.2 4.5 %copy-start = (bf16[240,1600]{1,0:T(8,128)(2,1)}, bf16[240,1600]{1,0:T(8,128)(2,1)S(1)}, u32[]{:S(2)}) copy-start(bf16[240,1600]{1,0:T(8,128)(2,1)S(1)} %multiply_convert_fusion.refs_1_.gated_ref) | copy-start | bytes 2304004
  141.2 5.8 %slice-start = ((bf16[240,1600]{1,0:T(8,128)(2,1)}), bf16[240,384]{1,0:T(8,128)(2,1)S(1)}, s32[]{:S(2)}) async-start(bf16[240,1600]{1,0:T(8,128)(2,1)} %copy-done.9), calls=%async_computation | async-start | bytes 368640 | tf_op jit(solution)/shard_map/slice | solution.py:406
  145.7 37.6 %collective-permute-start.8 = (bf16[800,896]{1,0:T(8,128)(2,1)}, bf16[800,896]{1,0:T(8,128)(2,1)}, u32[]{:S(2)}, u32[]{:S(2)}) collective-permute-start(bf16[800,896]{1,0:T(8,128)(2,1)} %shard_map.125), channel_id=1, source_target_pairs={{0,1},{1,0},{2,3},{3,2},{4,5},{5,4},{6,7},{7,6},{8,9},{9,8},{10,11... | collective-permute-start | bytes 4300808 | tf_op jit(solution)/shard_map/ppermute | solution.py:29
  146.0 3.9 %copy-start.1 = (bf16[240,1600]{1,0:T(8,128)(2,1)S(1)}, bf16[240,1600]{1,0:T(8,128)(2,1)}, u32[]{:S(2)}) copy-start(bf16[240,1600]{1,0:T(8,128)(2,1)} %copy-done) | copy-start | bytes 2304004
  147.1 18.2 %collective-permute-start.6 = (bf16[480,384]{1,0:T(8,128)(2,1)S(1)}, bf16[480,384]{1,0:T(8,128)(2,1)S(1)}, u32[]{:S(2)}, u32[]{:S(2)}) collective-permute-start(bf16[480,384]{1,0:T(8,128)(2,1)S(1)} %pad_maximum_fusion.1), channel_id=1, source_target_pairs={{0,30},{2,28},{4,26},{6,24},{8,22},{10,20},{12,18},{14,16},{16,14}... | collective-permute-start | bytes 1105928 | tf_op jit(solution)/shard_map/ppermute | solution.py:25
  147.3 22.2 %collective-permute-start.11 = (bf16[1,1600]{1,0:T(2,128)(2,1)S(1)}, bf16[1,1600]{1,0:T(2,128)(2,1)S(1)}, u32[]{:S(2)}, u32[]{:S(2)}) collective-permute-start(bf16[1,1600]{1,0:T(2,128)(2,1)S(1)} %add_convert_fusion), channel_id=1, source_target_pairs={{0,30},{2,28},{4,26},{6,24},{8,22},{10,20},{12,18},{14,16},{16,14}... | collective-permute-start | bytes 9608 | tf_op jit(solution)/shard_map/ppermute | solution.py:25
  149.9 1.1 copy-start.14
  151.0 14.3 %copy-start.4 = (bf16[240,1600]{1,0:T(8,128)(2,1)S(1)}, bf16[240,1600]{1,0:T(8,128)(2,1)}, u32[]{:S(2)}) copy-start(bf16[240,1600]{1,0:T(8,128)(2,1)} %copy-done.2) | copy-start | bytes 2304004
  158.2 10.8 %slice-start.1 = ((bf16[240,1600]{1,0:T(8,128)(2,1)}), bf16[240,320]{1,0:T(8,128)(2,1)S(1)}, s32[]{:S(2)}) async-start(bf16[240,1600]{1,0:T(8,128)(2,1)} %copy-done.9), calls=%async_computation.1 | async-start | bytes 368640 | tf_op jit(solution)/shard_map/slice | solution.py:406
  166.8 25.8 %collective-permute-start.10 = (bf16[800,384]{1,0:T(8,128)(2,1)S(1)}, bf16[800,384]{1,0:T(8,128)(2,1)S(1)}, u32[]{:S(2)}, u32[]{:S(2)}) collective-permute-start(bf16[800,384]{1,0:T(8,128)(2,1)S(1)} %shard_map.126), channel_id=1, source_target_pairs={{0,1},{1,0},{2,3},{3,2},{4,5},{5,4},{6,7},{7,6},{8,9},{9,8},{10,11... | collective-permute-start | bytes 1843208 | tf_op jit(solution)/shard_map/ppermute | solution.py:29
  169.1 14.2 %collective-permute-start.7 = (bf16[480,320]{1,0:T(8,128)(2,1)S(1)}, bf16[480,320]{1,0:T(8,128)(2,1)S(1)}, u32[]{:S(2)}, u32[]{:S(2)}) collective-permute-start(bf16[480,320]{1,0:T(8,128)(2,1)S(1)} %pad_maximum_fusion.2), channel_id=1, source_target_pairs={{0,30},{2,28},{4,26},{6,24},{8,22},{10,20},{12,18},{14,16},{16,14}... | collective-permute-start | bytes 921608 | tf_op jit(solution)/shard_map/ppermute | solution.py:25
  184.7 20.5 %collective-permute-start.9 = (bf16[800,384]{1,0:T(8,128)(2,1)S(1)}, bf16[800,384]{1,0:T(8,128)(2,1)S(1)}, u32[]{:S(2)}, u32[]{:S(2)}) collective-permute-start(bf16[800,384]{1,0:T(8,128)(2,1)S(1)} %shard_map.127), channel_id=1, source_target_pairs={{0,1},{1,0},{2,3},{3,2},{4,5},{5,4},{6,7},{7,6},{8,9},{9,8},{10,11... | collective-permute-start | bytes 1843208 | tf_op jit(solution)/shard_map/ppermute | solution.py:29
  185.1 19.5 %collective-permute-start.12 = (bf16[800]{0:T(1024)(128)(2,1)S(1)}, bf16[800]{0:T(1024)(128)(2,1)S(1)}, u32[]{:S(2)}, u32[]{:S(2)}) collective-permute-start(bf16[800]{0:T(1024)(128)(2,1)S(1)} %fusion.20), channel_id=1, source_target_pairs={{0,1},{1,0},{2,3},{3,2},{4,5},{5,4},{6,7},{7,6},{8,9},{9,8},{10,11... | collective-permute-start | bytes 4808 | tf_op jit(solution)/shard_map/ppermute | solution.py:29
where the time goes:
time: 209 us; the launch traced here: 208 us
  waiting for transfers between devices  87.1 us (42%)
  Pallas kernels  50.4 us (24%)
  local copies, waits for them, and re-layouts  34.3 us (16%)
  starting transfers between devices  21.6 us (10%)
  other arithmetic  13.1 us (6%)
    ppermute x6, waiting for transfers between devices, swapped(): return lax.ppermute(shard, 'dp', [(0, 1), (1, 0)])  61.6 us
    pallas_call x6, Pallas kernels, section_call(): pl.pallas_call(kernel, out_shape=[shapes[out] for out in outs], in_specs=...  33 us
    ppermute x5, waiting for transfers between devices, mirrored(): return lax.ppermute(shard, 'pipe', [(i, size - 1 - i) for i in range(size)])  22 us
    unnamed x69, local copies, waits for them, and re-layouts  19.5 us
    pallas_call x6, Pallas kernels, product_call(): pl.pallas_call(kernel, out_shape=out_shape, grid_spec=pltpu.PrefetchScala...  17.4 us
    ppermute x2, starting transfers between devices, shifted(): return lax.ppermute(shard, 'pipe', pairs)  9.27 us
    ppermute x5, starting transfers between devices, mirrored(): return lax.ppermute(shard, 'pipe', [(i, size - 1 - i) for i in range(size)])  7.6 us
    optimization_barrier x2, local copies, waits for them, and re-layouts, after(): return lax.optimization_barrier((value, *earlier))[0]  6.01 us
  transfers between devices with their start and end apart: 13, of which 9 were waited for; matrix products, arithmetic and copies ran while one was open for 15% of the time, Pallas kernels for 21%

commit v1 on v0

--- a/solution.py
+++ b/solution.py
@@ -101,8 +101,11 @@
         )
 
 
-def settle_back(rows_ref, cot_ref, gain_ref, back, passed_ref, term_ref):
-    whitened, inv_std = whiten(rows_ref[...])
+def settle_back(rows_ref, cot_ref, gain_ref, back, passed_ref, term_ref, white=None):
+    if white is None:
+        whitened, inv_std = whiten(rows_ref[...])
+    else:
+        whitened, inv_std = white[0][...], white[1]
     term_ref[...] = jnp.sum(back[...] * whitened, axis=0, keepdims=True)
     scaled = back[...] * gain_ref[...].astype(jnp.float32)
     mean_back = jnp.mean(scaled, axis=-1, keepdims=True)
@@ -124,15 +127,16 @@
 
 def step_kernel(
     rank_ref, rows_ref, normed_ref, cot_ref, gain_ref, own_ref, far_ref,
-    gated_ref, passed_ref, term_ref, weight, sems, back,
+    gated_ref, passed_ref, term_ref, weight, sems, back, white,
 ):
     pairs = fetch(rank_ref, own_ref, far_ref, weight, sems)
+    white[...], inv_std = whiten(rows_ref[...])
     for pair, (lo, hi) in zip(pairs, column_pieces(gated_ref.shape[1])):
         wait_for(pair)
         slope = slope_piece(normed_ref, weight, lo, hi)
         gated_ref[:, lo:hi] = (cot_ref[:, lo:hi].astype(jnp.float32) * slope).astype(jnp.bfloat16)
     fill_back(gated_ref, weight, back)
-    settle_back(rows_ref, cot_ref, gain_ref, back, passed_ref, term_ref)
+    settle_back(rows_ref, cot_ref, gain_ref, back, passed_ref, term_ref, (white, inv_std))
 
 
 def section_call(kernel, rank, operands, halves, outs, cost):
@@ -147,8 +151,7 @@
         pltpu.VMEM((width, width), jnp.bfloat16),
         pltpu.SemaphoreType.DMA((len(column_pieces(width)), 2)),
     ]
-    if "term" in outs:
-        scratch.append(pltpu.VMEM((tokens, width), jnp.float32))
+    scratch += [pltpu.VMEM((tokens, width), jnp.float32)] * (len(outs) - 1)
     return pl.pallas_call(
         kernel,
         out_shape=[shapes[out] for out in outs],
@@ -246,16 +249,15 @@
 def column_chunks(width):
     lane = 128
     tiles = -(-width // lane)
-    first = -(-tiles // 2)
-    second = first + (tiles - first) // 2
-    edges = [0, first * lane, second * lane, width]
+    edges = [0, -(-tiles // 6), -(-tiles // 2), tiles - tiles // 4]
+    edges = [edge * lane for edge in edges] + [width]
     return list(zip(edges, edges[1:]))
 
 
-def gather_gates(gate_refs, lo, span, stack, sems):
+def gather_gates(gate_refs, starts, span, stack, sems):
     copies = []
     row = 0
-    for k, ref in enumerate(gate_refs):
+    for k, (ref, lo) in enumerate(zip(gate_refs, starts)):
         rows, width = ref.shape
         source = ref if width == span else ref.at[:, lo : lo + span]
         copies.append(
@@ -268,12 +270,12 @@
         copy.wait()
 
 
-def send_kernel(lo, span, rank_ref, turned_ref, *refs):
+def send_kernel(starts, span, rank_ref, turned_ref, *refs):
     *gate_refs, part_ref, stack, sems = refs
 
     @pl.when(pl.program_id(0) == 0)
     def _():
-        gather_gates(gate_refs, lo, span, stack, sems)
+        gather_gates(gate_refs, starts, span, stack, sems)
 
     part_ref[:, :span] = jnp.dot(
         turned_ref[...], stack[...], preferred_element_type=jnp.float32
@@ -283,7 +285,8 @@
         part_ref[:, span:] = jnp.zeros(spare, jnp.bfloat16)
 
 
-def keep_kernel(lo, span, count, grown, rank_ref, turned_ref, arrived_ref, *refs):
+def keep_kernel(lo, starts, span, grown, rank_ref, turned_ref, arrived_ref, *refs):
+    count = len(starts)
     gate_refs = refs[:count]
     out_ref, stack, total, sems, out_sems = refs[count + (1 if grown else 0) :]
     step = pl.program_id(0)
@@ -291,7 +294,7 @@
 
     @pl.when(step == 0)
     def _():
-        gather_gates(gate_refs, lo, span, stack, sems)
+        gather_gates(gate_refs, starts, span, stack, sems)
 
     total[step] = jnp.dot(
         turned_ref[...], stack[...], preferred_element_type=jnp.float32
@@ -310,7 +313,9 @@
             put(i).wait()
 
 
-def product_call(rank, turned, gates, lo, hi, arrived=None, grown=None):
+def product_call(rank, turned, placed, lo, hi, arrived=None, grown=None):
+    gates = [gate for gate, _ in placed]
+    starts = [start for _, start in placed]
     width, depth = turned.shape
     half, span = width // 2, hi - lo
     padded = lanes(span)
@@ -333,12 +338,12 @@
     scratch = [pltpu.VMEM((depth, span), jnp.bfloat16)]
     aliases = {}
     if sending:
-        kernel = functools.partial(send_kernel, lo, span)
+        kernel = functools.partial(send_kernel, starts, span)
         out_shape = jax.ShapeDtypeStruct((half, padded), jnp.bfloat16)
         out_spec = pl.BlockSpec((rows, padded), lambda i, rank_ref: (i, 0))
         scratch += [pltpu.SemaphoreType.DMA((len(gates),))]
     else:
-        kernel = functools.partial(keep_kernel, lo, span, len(gates), grown is not None)
+        kernel = functools.partial(keep_kernel, lo, starts, span, grown is not None)
         out_shape = jax.ShapeDtypeStruct((half, width), jnp.float32)
         out_spec = any_space
         scratch += [
@@ -405,7 +410,7 @@
     def columns(gates, lo, hi):
         return jnp.concatenate([gated[:, lo:hi] for gated in gates], axis=0)
 
-    moved = [mirrored(columns(gated_up, *chunks[0]))]
+    early = mirrored(columns(gated_up, 0, chunks[1][1]))
     up_last, term = back(
         rank, up_inputs[0, -1], cot_up, up_gain, gated_up[-1], halves_up
     )
@@ -423,28 +428,32 @@
         gated_down.append(gated)
         down_term = down_term + term
         cot_down = shifted(passed, -1)
-    slope_down = slope_of(rank, after(normed_down[-1], passed, moved), halves_down)
+    slope_down = slope_of(rank, after(normed_down[-1], passed, early), halves_down)
     gated_down.append(gated_by(after(cot_down, slope_down), slope_down))
 
     arrived = []
     gates = []
+    parts = []
     part = gated_down[-1]
     for i, (lo, hi) in enumerate(chunks):
-        if i > 0:
-            source = after(gated_up, cot_down if i == 1 else part)
-            moved.append(mirrored(columns(source, lo, hi)))
+        if i < 2:
+            piece, start = early, lo
+        else:
+            source = after(gated_up, parts[i - 2])
+            piece, start = mirrored(columns(source, lo, hi)), 0
         ready = [part] + arrived[max(i - 2, 0) : max(i - 1, 0)]
-        gates.append(gated_down + [after(moved[i], *ready)])
+        gates.append([(gated, lo) for gated in gated_down] + [(after(piece, *ready), start)])
         part = product_call(rank, turned, gates[i], lo, hi)
+        parts.append(part)
         arrived.append(swapped(part))
-        if i == 0:
+        if i == 1:
             down_last, term = back(
                 rank, down_inputs[0, -1], cot_down, down_gain, after(gated_down[-1], part),
                 halves_down,
             )
-            gain_sum = (down_term + term + mirror_term.astype(jnp.float32))[0]
-            gain_keep = jnp.where(first, gain_sum[:half], gain_sum[half:])
-            gain_send = jnp.where(first, gain_sum[half:], gain_sum[:half])
+            gain_sum = down_term + term + mirror_term.astype(jnp.float32)
+            gain_keep = jnp.where(first, gain_sum[:, :half], gain_sum[:, half:])
+            gain_send = jnp.where(first, gain_sum[:, half:], gain_sum[:, :half])
             gain_got = swapped(gain_send.astype(jnp.bfloat16))
     weight_out = None
     for i, (lo, hi) in enumerate(chunks):
@@ -452,7 +461,7 @@
             gain_got = after(gain_got, weight_out)
         weight_out = product_call(rank, turned, gates[i], lo, hi, arrived[i], weight_out)
     gain_out = gain_keep + gain_got.astype(jnp.float32)
-    return (weight_out[None], gain_out[None], down_last[None], up_last[None])
+    return (weight_out[None], gain_out, down_last[None], up_last[None])
 
 
 def local_many(

time: 209 us -> 207 us (level)
  waiting for transfers between devices: 87.1 us -> 83.8 us
    ppermute x5, waiting for transfers between devices: 22 us -> 17.2 us  [mirrored(): return lax.ppermute(shard, 'pipe', [(i, size - 1 - i) for i in range(size)])]
    ppermute x6 -> x7, waiting for transfers between devices: 61.6 us -> 63.1 us  [swapped(): return lax.ppermute(shard, 'dp', [(0, 1), (1, 0)])]
    ppermute x6 -> x7, starting transfers between devices: 4.72 us -> 5.97 us  [swapped(): return lax.ppermute(shard, 'dp', [(0, 1), (1, 0)])]
    unnamed x69 -> x63, local copies, waits for them, and re-layouts: 19.5 us -> 18.3 us
    pallas_call x6 -> x8, Pallas kernels: 17.4 us -> 18.2 us  [product_call(): pl.pallas_call(kernel, out_shape=out_shape, grid_spec=pltpu.PrefetchScala...]
  transfers between devices with their start and end apart: 13 -> 14, of which waited for: 9 -> 9; matrix products, arithmetic and copies ran while one was open for 15% -> 15% of each run, Pallas kernels for 21% -> 23%
where the time goes in v1:
time: 207 us; the launch traced here: 205 us
  waiting for transfers between devices  83.8 us (40%)
  Pallas kernels  51.3 us (25%)
  local copies, waits for them, and re-layouts  32.4 us (16%)
  starting transfers between devices  22.8 us (11%)
  other arithmetic  13.6 us (7%)
    ppermute x7, waiting for transfers between devices, swapped(): return lax.ppermute(shard, 'dp', [(0, 1), (1, 0)])  63.1 us
    pallas_call x6, Pallas kernels, section_call(): pl.pallas_call(kernel, out_shape=[shapes[out] for out in outs], in_specs=...  33 us
    unnamed x63, local copies, waits for them, and re-layouts  18.3 us
    pallas_call x8, Pallas kernels, product_call(): pl.pallas_call(kernel, out_shape=out_shape, grid_spec=pltpu.PrefetchScala...  18.2 us
    ppermute x5, waiting for transfers between devices, mirrored(): return lax.ppermute(shard, 'pipe', [(i, size - 1 - i) for i in range(size)])  17.2 us
    ppermute x2, starting transfers between devices, shifted(): return lax.ppermute(shard, 'pipe', pairs)  9.27 us
    ppermute x5, starting transfers between devices, mirrored(): return lax.ppermute(shard, 'pipe', [(i, size - 1 - i) for i in range(size)])  7.55 us
    optimization_barrier x2, local copies, waits for them, and re-layouts, after(): return lax.optimization_barrier((value, *earlier))[0]  6.03 us
  transfers between devices with their start and end apart: 14, of which 9 were waited for; matrix products, arithmetic and copies ran while one was open for 15% of the time, Pallas kernels for 23%

profile of v1, /device:TPU:15, one launch (start us, length us, event | category | flops | bytes accessed | tf_op | source)
XLA Modules:
  0.0 205.2 jit_solution(15568738886062379304)
XLA Ops:
  0.9 1.9 convert_reduce_fusion
  2.8 0.6 fusion.3
  3.5 1.7 fusion.5
  5.2 2.0 collective-permute-start.2
  7.2 2.5 %bitcast_select_fusion = (bf16[240,1600]{1,0:T(8,128)(2,1)}, bf16[240,1600]{1,0:T(8,128)(2,1)S(1)}) fusion(bf16[1,240,1600]{2,1,0:T(8,128)(2,1)} %param.15, pred[240]{0:T(512)(128)(4,1)S(1)} %get-tuple-element.68, bf16[1,240,1600]{2,1,0:T(8,128)(2,1)} %param.16, pred[240]{0:T(512)(128)(4,1)S(1)} %get-tuple-element.69), kind=kLoop, calls=%fused_computation.32 | loop fusion | flops 768000 | bytes 3072480 | tf_op jit(solution)/shard_map/jit(_where)/select_n | solution.py:200
  9.6 1.2 collective-permute-start
  10.9 3.6 %copy.22 = bf16[1,2,240,1600]{2,3,1,0:T(8,128)(2,1)} copy(bf16[1,2,240,1600]{3,2,1,0:T(8,128)(2,1)} %param.13) | data formatting | bytes 3072000 | tf_op args[4]
  14.5 1.6 slice_bitcast_fusion.3
  16.3 1.3 slice_bitcast_fusion.4
  17.6 0.7 copy-done.25
  18.3 1.0 slice_bitcast_fusion.6
  19.3 40.3 %collective-permute-done.1.far_ref = bf16[800,1600]{1,0:T(8,128)(2,1)S(1)} collective-permute-done((bf16[800,1600]{1,0:T(8,128)(2,1)}, bf16[800,1600]{1,0:T(8,128)(2,1)S(1)}, u32[]{:S(2)}, u32[]{:S(2)}) %collective-permute-start.1) | collective-permute-done | bytes 2560032 | tf_op jit(solution)/shard_map/ppermute | solution.py:29
  59.6 6.9 %shard_map.120 = (bf16[240,1600]{1,0:T(8,128)(2,1)S(1)}, bf16[240,1600]{1,0:T(8,128)(2,1)}, f32[1,1600]{1,0:T(1,128)S(1)}) custom-call(s32[1]{0:T(128)} %bitcast.rank_ref, bf16[240,1600]{1,0:T(8,128)(2,1)S(1)} %get-tuple-element.77.rows_ref, bf16[240,1600]{1,0:T(8,128)(2,1)S(1)} %get-tuple-element.78.normed_ref, ...), custom_call_target="tpu_custom_call" | custom-call | tf_op jit(solution)/shard_map/pallas_call | solution.py:155
  66.6 5.8 %collective-permute-start.3 = (bf16[240,1600]{1,0:T(8,128)(2,1)}, bf16[240,1600]{1,0:T(8,128)(2,1)S(1)}, u32[]{:S(2)}, u32[]{:S(2)}) collective-permute-start(bf16[240,1600]{1,0:T(8,128)(2,1)} %get-tuple-element.35), channel_id=1, source_target_pairs={{0,2},{2,4},{4,6},{6,8},{8,10},{10,12},{12,14},{14,16},{16,18},{18... | collective-permute-start | bytes 2304008 | tf_op jit(solution)/shard_map/ppermute | solution.py:20
  72.4 3.3 %shard_map.121 = f32[240,1600]{1,0:T(8,128)S(1)} custom-call(s32[1]{0:T(128)} %bitcast.rank_ref, bf16[240,1600]{1,0:T(8,128)(2,1)S(1)} %get-tuple-element.37.normed_ref, bf16[800,1600]{1,0:T(8,128)(2,1)S(1)} %bitcast.73, bf16[800,1600]{1,0:T(8,128)(2,1)S(1)} %collective-permute-done.1.far_ref), custom_call_target="tpu_custom_call" | custom-call | tf_op jit(solution)/shard_map/pallas_call | solution.py:155
  75.7 1.2 copy-done.8
  76.9 0.3 convert_reduce_fusion.2
  77.3 0.8 collective-permute-done.2
  78.1 3.6 %copy.23 = bf16[2,240,1600]{1,2,0:T(8,128)(2,1)} copy(bf16[2,240,1600]{2,1,0:T(8,128)(2,1)} %collective-permute-done.2) | data formatting | bytes 3072000 | tf_op jit(solution)/shard_map/optimization_barrier | solution.py:33
  81.6 0.5 fusion.9
  82.1 0.9 copy-done.28
  83.2 1.0 copy-done.19
  84.3 0.5 fusion.11
  84.9 0.8 copy-done.9
  85.9 0.7 copy-done.15
  86.6 1.0 pad_maximum_fusion
  87.6 2.5 %collective-permute-start.5 = (bf16[480,896]{1,0:T(8,128)(2,1)}, bf16[480,896]{1,0:T(8,128)(2,1)}, u32[]{:S(2)}, u32[]{:S(2)}) collective-permute-start(bf16[480,896]{1,0:T(8,128)(2,1)} %pad_maximum_fusion), channel_id=1, source_target_pairs={{0,30},{2,28},{4,26},{6,24},{8,22},{10,20},{12,18},{14,16},{16,14}... | collective-permute-start | bytes 2580488 | tf_op jit(solution)/shard_map/ppermute | solution.py:25
  90.0 2.4 %maximum_bitcast_fusion.turned_ref = bf16[1600,960]{1,0:T(8,128)(2,1)S(1)} fusion(bf16[240,1600]{0,1:T(8,128)(2,1)S(1)} %get-tuple-element.73, bf16[240,1600]{0,1:T(8,128)(2,1)S(1)} %get-tuple-element.72, bf16[240,1600]{0,1:T(8,128)(2,1)S(1)} %get-tuple-element.47, bf16[240,1600]{0,1:T(8,128)(2,1)S(1)} %get-tuple-element.70), kind=kLoop, calls=%fused_computation.2 | loop fusion | flops 12288000 | bytes 6144000 | tf_op jit(solution)/shard_map/transpose | solution.py:418
  92.4 2.2 %copy.25.normed_ref = bf16[240,1600]{1,0:T(8,128)(2,1)} copy(bf16[240,1600]{0,1:T(8,128)(2,1)} %copy-done.27) | data formatting | bytes 1536000 | tf_op jit(solution)/shard_map/convert_element_type | solution.py:52
  94.6 1.7 copy-done.3
  96.3 1.7 copy-done.5
  98.1 1.1 copy-done.7
  99.2 1.1 copy-done.14
  100.4 1.1 copy-done.16
  101.5 4.1 %shard_map.122 = (bf16[240,1600]{1,0:T(8,128)(2,1)}, f32[1,1600]{1,0:T(1,128)S(1)}) custom-call(s32[1]{0:T(128)} %bitcast.rank_ref, bf16[240,1600]{1,0:T(8,128)(2,1)S(1)} %copy-done.14, bf16[240,1600]{1,0:T(8,128)(2,1)S(1)} %copy-done.16, bf16[1,1600]{1,0:T(2,128)(2,1)S(1)} %copy-done.20, bf16[240,1600]{1,0:T(8,128)(2,1)S(1)} %copy-done.7, ...), custom_call_target="tpu_custom_call" | custom-call | tf_op jit(solution)/shard_map/pallas_call | solution.py:155
  105.6 11.1 %collective-permute-done.far_ref = bf16[800,1600]{1,0:T(8,128)(2,1)} collective-permute-done((bf16[800,1600]{1,0:T(8,128)(2,1)}, bf16[800,1600]{1,0:T(8,128)(2,1)}, u32[]{:S(2)}, u32[]{:S(2)}) %collective-permute-start) | collective-permute-done | bytes 2560032 | tf_op jit(solution)/shard_map/ppermute | solution.py:29
  116.7 7.4 %shard_map.123 = (bf16[240,1600]{1,0:T(8,128)(2,1)S(1)}, bf16[240,1600]{1,0:T(8,128)(2,1)}, f32[1,1600]{1,0:T(1,128)S(1)}) custom-call(s32[1]{0:T(128)} %bitcast.rank_ref, bf16[240,1600]{1,0:T(8,128)(2,1)S(1)} %copy-done.13, bf16[240,1600]{1,0:T(8,128)(2,1)S(1)} %copy-done.17, bf16[240,1600]{1,0:T(8,128)(2,1)S(1)} %copy-done.12, ...), custom_call_target="tpu_custom_call" | custom-call | tf_op jit(solution)/shard_map/pallas_call | solution.py:155
  124.1 0.9 copy-done
  125.0 3.4 %collective-permute-start.4 = (bf16[240,1600]{1,0:T(8,128)(2,1)}, bf16[240,1600]{1,0:T(8,128)(2,1)}, u32[]{:S(2)}, u32[]{:S(2)}) collective-permute-start(bf16[240,1600]{1,0:T(8,128)(2,1)} %get-tuple-element.45), channel_id=1, source_target_pairs={{2,0},{4,2},{6,4},{8,6},{10,8},{12,10},{14,12},{16,14},{18,16},{20... | collective-permute-start | bytes 2304008 | tf_op jit(solution)/shard_map/ppermute | solution.py:20
  128.5 2.5 %copy.26.normed_ref = bf16[240,1600]{1,0:T(8,128)(2,1)} copy(bf16[240,1600]{0,1:T(8,128)(2,1)} %copy-done.26) | data formatting | bytes 1536000 | tf_op jit(solution)/shard_map/optimization_barrier | solution.py:33
  130.9 1.1 copy-done.10
  132.0 4.2 %shard_map.124 = f32[240,1600]{1,0:T(8,128)S(1)} custom-call(s32[1]{0:T(128)} %bitcast.rank_ref, bf16[240,1600]{1,0:T(8,128)(2,1)S(1)} %copy-done.10, bf16[800,1600]{1,0:T(8,128)(2,1)} %bitcast.1.own_ref, bf16[800,1600]{1,0:T(8,128)(2,1)} %collective-permute-done.far_ref), custom_call_target="tpu_custom_call" | custom-call | tf_op jit(solution)/shard_map/pallas_call | solution.py:155
  136.3 3.4 %collective-permute-done.4.cot_ref = bf16[240,1600]{1,0:T(8,128)(2,1)} collective-permute-done((bf16[240,1600]{1,0:T(8,128)(2,1)}, bf16[240,1600]{1,0:T(8,128)(2,1)}, u32[]{:S(2)}, u32[]{:S(2)}) %collective-permute-start.4) | collective-permute-done | bytes 768032 | tf_op jit(solution)/shard_map/ppermute | solution.py:20
  139.7 1.3 multiply_convert_fusion.refs_1_.gated_ref
  141.0 2.3 %shard_map.125 = bf16[800,384]{1,0:T(8,128)(2,1)S(1)} custom-call(s32[1]{0:T(128)} %bitcast.rank_ref, bf16[1600,960]{1,0:T(8,128)(2,1)S(1)} %maximum_bitcast_fusion.turned_ref, bf16[240,1600]{1,0:T(8,128)(2,1)S(1)} %copy-done.1, bf16[240,1600]{1,0:T(8,128)(2,1)S(1)} %multiply_convert_fusion.refs_1_.gated_ref, bf16[480,896]{1,0:T(8,128)(2,1)} %collective-permute-done.5.refs_2_), custom_call_target="tpu_custom_call" | custom-call | flops 589824000 | bytes 5529600 | tf_op jit(solution)/shard_map/pallas_call | solution.py:358
  143.6 0.9 slice.61
  144.8 2.3 %shard_map.126 = bf16[800,512]{1,0:T(8,128)(2,1)S(1)} custom-call(s32[1]{0:T(128)} %bitcast.rank_ref, bf16[1600,960]{1,0:T(8,128)(2,1)S(1)} %maximum_bitcast_fusion.turned_ref, bf16[240,1600]{1,0:T(8,128)(2,1)S(1)} %copy-done.1, bf16[240,1600]{1,0:T(8,128)(2,1)S(1)} %multiply_convert_fusion.refs_1_.gated_ref, bf16[480,896]{1,0:T(8,128)(2,1)} %collective-permute-done.5.refs_2_), custom_call_target="tpu_custom_call" | custom-call | flops 786432000 | bytes 6348800 | tf_op jit(solution)/shard_map/pallas_call | solution.py:358
  147.1 1.3 collective-permute-start.9
  148.4 2.9 %collective-permute-start.12 = (bf16[1,1600]{1,0:T(2,128)(2,1)S(1)}, bf16[1,1600]{1,0:T(2,128)(2,1)S(1)}, u32[]{:S(2)}, u32[]{:S(2)}) collective-permute-start(bf16[1,1600]{1,0:T(2,128)(2,1)S(1)} %add_convert_fusion), channel_id=1, source_target_pairs={{0,30},{2,28},{4,26},{6,24},{8,22},{10,20},{12,18},{14,16},{16,14}... | collective-permute-start | bytes 9608 | tf_op jit(solution)/shard_map/ppermute | solution.py:25
  151.3 0.9 slice.59
  152.4 7.2 %shard_map.133 = (bf16[240,1600]{1,0:T(8,128)(2,1)}, f32[1,1600]{1,0:T(1,128)S(1)}) custom-call(s32[1]{0:T(128)} %bitcast.rank_ref, bf16[240,1600]{1,0:T(8,128)(2,1)S(1)} %copy-done.11, bf16[240,1600]{1,0:T(8,128)(2,1)} %collective-permute-done.4.cot_ref, bf16[1,1600]{1,0:T(2,128)(2,1)S(1)} %copy-done.21, ...), custom_call_target="tpu_custom_call" | custom-call | tf_op jit(solution)/shard_map/pallas_call | solution.py:155
  159.6 12.6 %collective-permute-done.7.refs_2_ = bf16[480,384]{1,0:T(8,128)(2,1)S(1)} collective-permute-done((bf16[480,384]{1,0:T(8,128)(2,1)S(1)}, bf16[480,384]{1,0:T(8,128)(2,1)S(1)}, u32[]{:S(2)}, u32[]{:S(2)}) %collective-permute-start.7) | collective-permute-done | bytes 368672 | tf_op jit(solution)/shard_map/ppermute | solution.py:25
  172.2 1.4 shard_map.127
  173.6 1.3 collective-permute-start.11
  174.9 3.8 %collective-permute-done.6.refs_2_ = bf16[480,320]{1,0:T(8,128)(2,1)S(1)} collective-permute-done((bf16[480,320]{1,0:T(8,128)(2,1)S(1)}, bf16[480,320]{1,0:T(8,128)(2,1)S(1)}, u32[]{:S(2)}, u32[]{:S(2)}) %collective-permute-start.6) | collective-permute-done | bytes 307232 | tf_op jit(solution)/shard_map/ppermute | solution.py:25
  178.7 1.4 shard_map.128
  180.2 1.3 collective-permute-start.10
  181.8 3.1 %shard_map.129.refs_3_ = f32[800,1600]{1,0:T(8,128)} custom-call(s32[1]{0:T(128)} %bitcast.rank_ref, bf16[1600,960]{1,0:T(8,128)(2,1)S(1)} %maximum_bitcast_fusion.turned_ref, bf16[800,384]{1,0:T(8,128)(2,1)S(1)} %collective-permute-done.8.arrived_ref, bf16[240,1600]{1,0:T(8,128)(2,1)S(1)} %copy-done.1, ...), custom_call_target="tpu_custom_call" | custom-call | flops 589824000 | bytes 5529600 | tf_op jit(solution)/shard_map/pallas_call | solution.py:358
  184.9 3.2 %shard_map.130.refs_3_ = f32[800,1600]{1,0:T(8,128)} custom-call(s32[1]{0:T(128)} %bitcast.rank_ref, bf16[1600,960]{1,0:T(8,128)(2,1)S(1)} %maximum_bitcast_fusion.turned_ref, bf16[800,512]{1,0:T(8,128)(2,1)S(1)} %collective-permute-done.9.arrived_ref, bf16[240,1600]{1,0:T(8,128)(2,1)S(1)} %copy-done.1, ...), custom_call_target="tpu_custom_call", output_to_operand_aliasing={{}: (6, {})} | custom-call | flops 786432000 | bytes 6348800 | tf_op jit(solution)/shard_map/pallas_call | solution.py:358
  188.1 1.4 collective-permute-done.11.arrived_ref
  189.4 2.3 %shard_map.131.refs_3_ = f32[800,1600]{1,0:T(8,128)} custom-call(s32[1]{0:T(128)} %bitcast.rank_ref, bf16[1600,960]{1,0:T(8,128)(2,1)S(1)} %maximum_bitcast_fusion.turned_ref, bf16[800,384]{1,0:T(8,128)(2,1)S(1)} %collective-permute-done.11.arrived_ref, bf16[240,1600]{1,0:T(8,128)(2,1)S(1)} %copy-done.1, ...), custom_call_target="tpu_custom_call", output_to_operand_aliasing={{}: (6, {})} | custom-call | flops 589824000 | bytes 5529600 | tf_op jit(solution)/shard_map/pallas_call | solution.py:358
  191.7 10.4 %collective-permute-done.13 = bf16[1,800]{1,0:T(2,128)(2,1)S(1)} collective-permute-done((bf16[1,800]{1,0:T(2,128)(2,1)S(1)}, bf16[1,800]{1,0:T(2,128)(2,1)S(1)}, u32[]{:S(2)}, u32[]{:S(2)}) %collective-permute-start.13) | collective-permute-done | bytes 1632 | tf_op jit(solution)/shard_map/ppermute | solution.py:29
  202.1 0.7 fusion.18
  202.7 2.3 %shard_map.132 = f32[800,1600]{1,0:T(8,128)} custom-call(s32[1]{0:T(128)} %bitcast.rank_ref, bf16[1600,960]{1,0:T(8,128)(2,1)S(1)} %maximum_bitcast_fusion.turned_ref, bf16[800,384]{1,0:T(8,128)(2,1)S(1)} %collective-permute-done.10.arrived_ref, bf16[240,1600]{1,0:T(8,128)(2,1)S(1)} %copy-done.1, ...), custom_call_target="tpu_custom_call", output_to_operand_aliasing={{}: (6, {})} | custom-call | flops 491520000 | bytes 5120000 | tf_op jit(solution)/shard_map/pallas_call | solution.py:358
  (82 shorter events, 2.1 us)
Async XLA Ops:
  0.6 2.2 %copy-start.24 = (bf16[1,2,240,1600]{3,2,1,0:T(8,128)(2,1)S(1)}, bf16[1,2,240,1600]{3,2,1,0:T(8,128)(2,1)}, u32[]{:S(2)}) copy-start(bf16[1,2,240,1600]{3,2,1,0:T(8,128)(2,1)} %param.14) | copy-start | bytes 4608004
  0.6 2.8 %copy-start.20 = (bf16[1,1600]{1,0:T(2,128)(2,1)S(1)}, bf16[1,1600]{1,0:T(2,128)(2,1)}, u32[]{:S(2)}) copy-start(bf16[1,1600]{1,0:T(2,128)(2,1)} %gain_ref.5) | copy-start | bytes 9604
  0.7 59.0 %collective-permute-start.1 = (bf16[800,1600]{1,0:T(8,128)(2,1)}, bf16[800,1600]{1,0:T(8,128)(2,1)S(1)}, u32[]{:S(2)}, u32[]{:S(2)}) collective-permute-start(bf16[800,1600]{1,0:T(8,128)(2,1)} %bitcast.71), channel_id=1, source_target_pairs={{0,1},{1,0},{2,3},{3,2},{4,5},{5,4},{6,7},{7,6},{8,9},{9,8},{10,11... | collective-permute-start | bytes 7680008 | tf_op jit(solution)/shard_map/ppermute | solution.py:29
  3.4 3.7 %copy-start.30 = (s32[2,240]{1,0:T(2,128)S(1)}, s32[2,240]{1,0:T(2,128)}, u32[]{:S(2)}) copy-start(s32[2,240]{1,0:T(2,128)} %param.17) | copy-start | bytes 5764
  5.2 72.9 %collective-permute-start.2 = (bf16[2,240,1600]{2,1,0:T(8,128)(2,1)}, bf16[2,240,1600]{2,1,0:T(8,128)(2,1)}, u32[]{:S(2)}, u32[]{:S(2)}) collective-permute-start(bf16[2,240,1600]{2,1,0:T(8,128)(2,1)} %fusion.5), channel_id=1, source_target_pairs={{0,30},{2,28},{4,26},{6,24},{8,22},{10,20},{12,18},{14,16},{16,14}... | collective-permute-start | bytes 4608008 | tf_op jit(solution)/shard_map/ppermute | solution.py:25
  9.6 4.8 %copy-start.21 = (bf16[1,1600]{1,0:T(2,128)(2,1)S(1)}, bf16[1,1600]{1,0:T(2,128)(2,1)}, u32[]{:S(2)}) copy-start(bf16[1,1600]{1,0:T(2,128)(2,1)} %gain_ref.7) | copy-start | bytes 9604
  9.6 107.1 %collective-permute-start = (bf16[800,1600]{1,0:T(8,128)(2,1)}, bf16[800,1600]{1,0:T(8,128)(2,1)}, u32[]{:S(2)}, u32[]{:S(2)}) collective-permute-start(bf16[800,1600]{1,0:T(8,128)(2,1)} %bitcast.1.own_ref), channel_id=1, source_target_pairs={{0,1},{1,0},{2,3},{3,2},{4,5},{5,4},{6,7},{7,6},{8,9},{9,8},{10,11... | collective-permute-start | bytes 7680008 | tf_op jit(solution)/shard_map/ppermute | solution.py:29
  14.4 1.9 copy-start.29
  16.3 2.0 copy-start.25
  18.3 41.3 %copy-start.2 = (bf16[1,800,1600]{2,1,0:T(8,128)(2,1)S(1)}, bf16[1,800,1600]{2,1,0:T(8,128)(2,1)}, u32[]{:S(2)}) copy-start(bf16[1,800,1600]{2,1,0:T(8,128)(2,1)} %param.10) | copy-start | bytes 7680004
  59.6 12.7 %copy-start.4 = (bf16[800,1600]{1,0:T(8,128)(2,1)}, bf16[800,1600]{1,0:T(8,128)(2,1)S(1)}, u32[]{:S(2)}) copy-start(bf16[800,1600]{1,0:T(8,128)(2,1)S(1)} %collective-permute-done.1.far_ref) | copy-start | bytes 7680004
  66.5 9.1 %copy-start.18 = (bf16[240,1600]{1,0:T(8,128)(2,1)}, bf16[240,1600]{1,0:T(8,128)(2,1)S(1)}, u32[]{:S(2)}) copy-start(bf16[240,1600]{1,0:T(8,128)(2,1)S(1)} %get-tuple-element.51) | copy-start | bytes 2304004
  66.6 18.3 %collective-permute-start.3 = (bf16[240,1600]{1,0:T(8,128)(2,1)}, bf16[240,1600]{1,0:T(8,128)(2,1)S(1)}, u32[]{:S(2)}, u32[]{:S(2)}) collective-permute-start(bf16[240,1600]{1,0:T(8,128)(2,1)} %get-tuple-element.35), channel_id=1, source_target_pairs={{0,2},{2,4},{4,6},{6,8},{8,10},{10,12},{12,14},{14,16},{16,18},{18... | collective-permute-start | bytes 2304008 | tf_op jit(solution)/shard_map/ppermute | solution.py:20
  72.4 4.5 %copy-start.22 = (bf16[1,2,240,1600]{2,3,1,0:T(8,128)(2,1)S(1)}, bf16[1,2,240,1600]{2,3,1,0:T(8,128)(2,1)}, u32[]{:S(2)}) copy-start(bf16[1,2,240,1600]{2,3,1,0:T(8,128)(2,1)} %copy.22) | copy-start | bytes 4608004
  75.7 1.3 copy-start.8
  77.3 4.4 %copy-start.23 = (bf16[1,2,240,1600]{2,3,1,0:T(8,128)(2,1)S(1)}, bf16[1,2,240,1600]{2,3,1,0:T(8,128)(2,1)}, u32[]{:S(2)}) copy-start(bf16[1,2,240,1600]{2,3,1,0:T(8,128)(2,1)} %copy.22) | copy-start | bytes 4608004
  81.6 1.4 copy-start.28
  83.1 1.1 copy-start.19
  84.3 1.4 copy-start.9
  84.8 5.2 %copy-start.26 = (bf16[240,1600]{0,1:T(8,128)(2,1)}, bf16[240,1600]{0,1:T(8,128)(2,1)S(1)}, u32[]{:S(2)}) copy-start(bf16[240,1600]{0,1:T(8,128)(2,1)S(1)} %get-tuple-element.47) | copy-start | bytes 2304004
  84.8 5.2 %copy-start.27 = (bf16[240,1600]{0,1:T(8,128)(2,1)}, bf16[240,1600]{0,1:T(8,128)(2,1)S(1)}, u32[]{:S(2)}) copy-start(bf16[240,1600]{0,1:T(8,128)(2,1)S(1)} %get-tuple-element.70) | copy-start | bytes 2304004
  85.7 0.9 copy-start.15
  85.8 4.2 %copy-start.6 = (bf16[240,1600]{1,0:T(8,128)(2,1)}, bf16[240,1600]{1,0:T(8,128)(2,1)S(1)}, u32[]{:S(2)}) copy-start(bf16[240,1600]{1,0:T(8,128)(2,1)S(1)} %multiply_convert_fusion.1.gated_ref) | copy-start | bytes 2304004
  87.6 40.9 %collective-permute-start.5 = (bf16[480,896]{1,0:T(8,128)(2,1)}, bf16[480,896]{1,0:T(8,128)(2,1)}, u32[]{:S(2)}, u32[]{:S(2)}) collective-permute-start(bf16[480,896]{1,0:T(8,128)(2,1)} %pad_maximum_fusion), channel_id=1, source_target_pairs={{0,30},{2,28},{4,26},{6,24},{8,22},{10,20},{12,18},{14,16},{16,14}... | collective-permute-start | bytes 2580488 | tf_op jit(solution)/shard_map/ppermute | solution.py:25
  94.6 1.8 copy-start.3
  96.3 1.8 copy-start.5
  98.1 1.1 copy-start.7
  99.2 1.1 copy-start.14
  100.4 1.1 copy-start.16
  101.5 15.2 %copy-start.12 = (bf16[240,1600]{1,0:T(8,128)(2,1)S(1)}, bf16[240,1600]{1,0:T(8,128)(2,1)}, u32[]{:S(2)}) copy-start(bf16[240,1600]{1,0:T(8,128)(2,1)} %get-tuple-element.42.cot_ref) | copy-start | bytes 2304004
  101.5 15.2 %copy-start.13 = (bf16[240,1600]{1,0:T(8,128)(2,1)S(1)}, bf16[240,1600]{1,0:T(8,128)(2,1)}, u32[]{:S(2)}) copy-start(bf16[240,1600]{1,0:T(8,128)(2,1)} %get-tuple-element.75.rows_ref) | copy-start | bytes 2304004
  101.5 15.2 %copy-start.17 = (bf16[240,1600]{1,0:T(8,128)(2,1)S(1)}, bf16[240,1600]{1,0:T(8,128)(2,1)}, u32[]{:S(2)}) copy-start(bf16[240,1600]{1,0:T(8,128)(2,1)} %copy.25.normed_ref) | copy-start | bytes 2304004
  124.1 0.9 copy-start
  125.0 14.7 %collective-permute-start.4 = (bf16[240,1600]{1,0:T(8,128)(2,1)}, bf16[240,1600]{1,0:T(8,128)(2,1)}, u32[]{:S(2)}, u32[]{:S(2)}) collective-permute-start(bf16[240,1600]{1,0:T(8,128)(2,1)} %get-tuple-element.45), channel_id=1, source_target_pairs={{2,0},{4,2},{6,4},{8,6},{10,8},{12,10},{14,12},{16,14},{18,16},{20... | collective-permute-start | bytes 2304008 | tf_op jit(solution)/shard_map/ppermute | solution.py:20
  130.9 1.1 copy-start.10
  136.3 4.7 %copy-start.1 = (bf16[240,1600]{1,0:T(8,128)(2,1)S(1)}, bf16[240,1600]{1,0:T(8,128)(2,1)}, u32[]{:S(2)}) copy-start(bf16[240,1600]{1,0:T(8,128)(2,1)} %copy-done) | copy-start | bytes 2304004
  141.0 3.6 %slice-start = ((bf16[240,1600]{1,0:T(8,128)(2,1)}), bf16[240,384]{1,0:T(8,128)(2,1)S(1)}, s32[]{:S(2)}) async-start(bf16[240,1600]{1,0:T(8,128)(2,1)} %copy-done.6), calls=%async_computation | async-start | bytes 368640 | tf_op jit(solution)/shard_map/slice | solution.py:411
  143.3 28.8 %collective-permute-start.8 = (bf16[800,384]{1,0:T(8,128)(2,1)S(1)}, bf16[800,384]{1,0:T(8,128)(2,1)S(1)}, u32[]{:S(2)}, u32[]{:S(2)}) collective-permute-start(bf16[800,384]{1,0:T(8,128)(2,1)S(1)} %shard_map.125), channel_id=1, source_target_pairs={{0,1},{1,0},{2,3},{3,2},{4,5},{5,4},{6,7},{7,6},{8,9},{9,8},{10,11... | collective-permute-start | bytes 1843208 | tf_op jit(solution)/shard_map/ppermute | solution.py:29
  144.6 7.6 %slice-start.1 = ((bf16[240,1600]{1,0:T(8,128)(2,1)}), bf16[240,320]{1,0:T(8,128)(2,1)S(1)}, s32[]{:S(2)}) async-start(bf16[240,1600]{1,0:T(8,128)(2,1)} %copy-done.6), calls=%async_computation.1 | async-start | bytes 368640 | tf_op jit(solution)/shard_map/slice | solution.py:411
  144.6 27.5 %collective-permute-start.7 = (bf16[480,384]{1,0:T(8,128)(2,1)S(1)}, bf16[480,384]{1,0:T(8,128)(2,1)S(1)}, u32[]{:S(2)}, u32[]{:S(2)}) collective-permute-start(bf16[480,384]{1,0:T(8,128)(2,1)S(1)} %pad_maximum_fusion.2), channel_id=1, source_target_pairs={{0,30},{2,28},{4,26},{6,24},{8,22},{10,20},{12,18},{14,16},{16,14}... | collective-permute-start | bytes 1105928 | tf_op jit(solution)/shard_map/ppermute | solution.py:25
  147.1 5.3 %copy-start.11 = (bf16[240,1600]{1,0:T(8,128)(2,1)S(1)}, bf16[240,1600]{1,0:T(8,128)(2,1)}, u32[]{:S(2)}) copy-start(bf16[240,1600]{1,0:T(8,128)(2,1)} %get-tuple-element.74.rows_ref) | copy-start | bytes 2304004
  147.1 31.6 %collective-permute-start.9 = (bf16[800,512]{1,0:T(8,128)(2,1)S(1)}, bf16[800,512]{1,0:T(8,128)(2,1)S(1)}, u32[]{:S(2)}, u32[]{:S(2)}) collective-permute-start(bf16[800,512]{1,0:T(8,128)(2,1)S(1)} %shard_map.126), channel_id=1, source_target_pairs={{0,1},{1,0},{2,3},{3,2},{4,5},{5,4},{6,7},{7,6},{8,9},{9,8},{10,11... | collective-permute-start | bytes 2457608 | tf_op jit(solution)/shard_map/ppermute | solution.py:29
  148.4 26.5 %collective-permute-start.12 = (bf16[1,1600]{1,0:T(2,128)(2,1)S(1)}, bf16[1,1600]{1,0:T(2,128)(2,1)S(1)}, u32[]{:S(2)}, u32[]{:S(2)}) collective-permute-start(bf16[1,1600]{1,0:T(2,128)(2,1)S(1)} %add_convert_fusion), channel_id=1, source_target_pairs={{0,30},{2,28},{4,26},{6,24},{8,22},{10,20},{12,18},{14,16},{16,14}... | collective-permute-start | bytes 9608 | tf_op jit(solution)/shard_map/ppermute | solution.py:25
  152.3 26.4 %collective-permute-start.6 = (bf16[480,320]{1,0:T(8,128)(2,1)S(1)}, bf16[480,320]{1,0:T(8,128)(2,1)S(1)}, u32[]{:S(2)}, u32[]{:S(2)}) collective-permute-start(bf16[480,320]{1,0:T(8,128)(2,1)S(1)} %pad_maximum_fusion.1), channel_id=1, source_target_pairs={{0,30},{2,28},{4,26},{6,24},{8,22},{10,20},{12,18},{14,16},{16,14}... | collective-permute-start | bytes 921608 | tf_op jit(solution)/shard_map/ppermute | solution.py:25
  173.6 15.9 %collective-permute-start.11 = (bf16[800,384]{1,0:T(8,128)(2,1)S(1)}, bf16[800,384]{1,0:T(8,128)(2,1)S(1)}, u32[]{:S(2)}, u32[]{:S(2)}) collective-permute-start(bf16[800,384]{1,0:T(8,128)(2,1)S(1)} %shard_map.127), channel_id=1, source_target_pairs={{0,1},{1,0},{2,3},{3,2},{4,5},{5,4},{6,7},{7,6},{8,9},{9,8},{10,11... | collective-permute-start | bytes 1843208 | tf_op jit(solution)/shard_map/ppermute | solution.py:29
  180.2 22.6 %collective-permute-start.10 = (bf16[800,384]{1,0:T(8,128)(2,1)S(1)}, bf16[800,384]{1,0:T(8,128)(2,1)S(1)}, u32[]{:S(2)}, u32[]{:S(2)}) collective-permute-start(bf16[800,384]{1,0:T(8,128)(2,1)S(1)} %shard_map.128), channel_id=1, source_target_pairs={{0,1},{1,0},{2,3},{3,2},{4,5},{5,4},{6,7},{7,6},{8,9},{9,8},{10,11... | collective-permute-start | bytes 1843208 | tf_op jit(solution)/shard_map/ppermute | solution.py:29
  181.6 20.5 %collective-permute-start.13 = (bf16[1,800]{1,0:T(2,128)(2,1)S(1)}, bf16[1,800]{1,0:T(2,128)(2,1)S(1)}, u32[]{:S(2)}, u32[]{:S(2)}) collective-permute-start(bf16[1,800]{1,0:T(2,128)(2,1)S(1)} %fusion.19), channel_id=1, source_target_pairs={{0,1},{1,0},{2,3},{3,2},{4,5},{5,4},{6,7},{7,6},{8,9},{9,8},{10,11... | collective-permute-start | bytes 4808 | tf_op jit(solution)/shard_map/ppermute | solution.py:29
